TPU v7x, 32 devices: a whole 2x2x4 slice. The times are simulated.
32 devices in a mesh: dp: 8 (over y, x, core), mp: 4 (over z).
Axes of the slice: x: 2, y: 2, z: 4, core: 2. Of those that a mesh axis runs over, the one named last changes fastest.
Arguments:
- hidden_in: bfloat16 [8192, 1024], P('dp'), may hold values from -6 to 6
- key_mask: int32 [8192], P('dp'), may hold values from 0 to 1, as said below
- bucket_of_offset: int32 [2047], replicated, may hold values from 0 to 511, as said below
- position_table: bfloat16 [512, 1024], replicated, may hold values from -6 to 6
- query_weight: bfloat16 [1024, 1024], P(None, 'mp'), may hold values from -0.1875 to 0.1875
- query_bias: bfloat16 [1024], P('mp'), may hold values from -3 to 3
- key_weight: bfloat16 [1024, 1024], P(None, 'mp'), may hold values from -0.1875 to 0.1875
- key_bias: bfloat16 [1024], P('mp'), may hold values from -3 to 3
- value_weight: bfloat16 [1024, 1024], P(None, 'mp'), may hold values from -0.1875 to 0.1875
- value_bias: bfloat16 [1024], P('mp'), may hold values from -3 to 3
- out_weight: bfloat16 [1024, 1024], P('mp'), may hold values from -3 to 3
- out_bias: bfloat16 [1024], replicated, may hold values from -3 to 3
- first_gain: bfloat16 [1024], replicated, may hold values from 0.5 to 1.5
- first_shift: bfloat16 [1024], replicated, may hold values from -1.75 to 1.75
- up_weight: bfloat16 [1024, 4096], P(None, 'mp'), may hold values from -0.1875 to 0.1875
- up_bias: bfloat16 [4096], P('mp'), may hold values from -3 to 3
- down_weight: bfloat16 [4096, 1024], P('mp'), may hold values from -0.09375 to 0.09375
- down_bias: bfloat16 [1024], replicated, may hold values from -3 to 3
- second_gain: bfloat16 [1024], replicated, may hold values from 0.5 to 1.5
- second_shift: bfloat16 [1024], replicated, may hold values from -1.75 to 1.75
- cotangent: bfloat16 [8192, 1024], P(('dp', 'mp')), may hold values from -6 to 6
Outputs:
- layer_out: bfloat16 [8192, 1024], P(('dp', 'mp'))
- input_grad: float32 [8192, 1024], P(('dp', 'mp'))
- table_grad: float32 [512, 1024], replicated
- query_weight_grad: float32 [1024, 1024], P(None, 'mp')
- query_bias_grad: float32 [1024], P('mp')
- key_weight_grad: float32 [1024, 1024], P(None, 'mp')
- key_bias_grad: float32 [1024], P('mp')
- value_weight_grad: float32 [1024, 1024], P(None, 'mp')
- value_bias_grad: float32 [1024], P('mp')
- out_weight_grad: float32 [1024, 1024], P('mp')
- out_bias_grad: float32 [1024], replicated
- first_gain_grad: float32 [1024], replicated
- first_shift_grad: float32 [1024], replicated
- up_weight_grad: float32 [1024, 4096], P(None, 'mp')
- up_bias_grad: float32 [4096], P('mp')
- down_weight_grad: float32 [4096, 1024], P('mp')
- down_bias_grad: float32 [1024], replicated
- second_gain_grad: float32 [1024], replicated
- second_shift_grad: float32 [1024], replicated
Inputs may be any that keep to these rules, and one draw needn't show every extreme that they name: `bucket_of_offset`: entry 1023 + o is the bucket of the offset o = i - j from key j to query i: it is 256 + o for |o| < min(128, 256), and never falls as o rises, by 0 or 1 a step. `key_mask`: in each sequence of 1024 tokens the ones form a prefix of 512 tokens or more, and its last token is 0.
All inputs are finite; a program needn't handle non-finite values.
Results may differ from a plain program's by a relative error of at most 0.029.
Values may be sent and summed in bfloat16 or wider, within the bound.
No kernel may reach another device: no remote copies, remote signals or barrier semaphores. Data moves between devices by JAX's collectives and lax.ppermute only.
A program may use at most 256 MiB of HBM per device.

v0:
```python
import math

import jax
import jax.numpy as jnp
from jax import lax
from jax.sharding import PartitionSpec as P

HEAD = 64
LEN = 1024


NORM_EPS = 1e-07
MASK_FILL = -1000000000.0


def norm_rows(values, gain_vec, shift_vec):
    row_mean = jnp.mean(values, axis=-1, keepdims=True)
    centered = values - row_mean
    row_var = jnp.mean(centered * centered, axis=-1, keepdims=True)
    return centered * lax.rsqrt(row_var + NORM_EPS) * gain_vec + shift_vec


def exact_gelu(values):
    return jax.nn.gelu(values, approximate=False)


def take_rows(values, start_at, row_count):
    return lax.dynamic_slice_in_dim(values, start_at, row_count, 0)


def add_rows(total_acc, part_rows, start_at):
    current = take_rows(total_acc, start_at, part_rows.shape[0])
    return lax.dynamic_update_slice_in_dim(total_acc, current + part_rows, start_at, 0)


def left_product(left_arr, right_arr):
    return lax.dot_general(
        left_arr, right_arr, (((0,), (0,)), ((), ())), preferred_element_type=jnp.float32
    )


def right_product(left_arr, right_arr):
    return lax.dot_general(
        left_arr, right_arr, (((1,), (1,)), ((), ())), preferred_element_type=jnp.float32
    )


def split_wide(values):
    upper_part = values.astype(jnp.bfloat16)
    lower_part = (values - upper_part.astype(jnp.float32)).astype(jnp.bfloat16)
    return (upper_part, lower_part)


def left_wide(narrow, wide_arr):
    upper_part, lower_part = split_wide(wide_arr)
    return left_product(narrow, upper_part) + left_product(narrow, lower_part)


def right_wide(wide_arr, narrow):
    upper_part, lower_part = split_wide(wide_arr)
    return right_product(upper_part, narrow) + right_product(lower_part, narrow)


def shear_rows(values, out_width):
    rows_n = values.shape[-2]
    amounts = rows_n - 1 - jnp.arange(rows_n, dtype=jnp.int32)
    current = values
    for bit_at in range(max(1, (rows_n - 1).bit_length())):
        step_size = 1 << bit_at
        filler = jnp.zeros(current.shape[:-1] + (step_size,), current.dtype)
        moved = jnp.concatenate([current[..., step_size:], filler], axis=-1)
        chosen = (amounts // step_size % 2 == 1)[:, None]
        current = jnp.where(chosen, moved, current)
    return current[..., :out_width]


def unshear_rows(grad_in, row_span):
    out_width = grad_in.shape[-1]
    zeros_in = jnp.zeros(grad_in.shape[:-1] + (row_span,), jnp.float32)
    _, pull_back = jax.vjp(lambda values: shear_rows(values, out_width), zeros_in)
    return pull_back(grad_in.astype(jnp.float32))[0]


def on_device(
    hidden_in,
    key_mask,
    bucket_of_offset,
    position_table,
    query_weight,
    query_bias,
    key_weight,
    key_bias,
    value_weight,
    value_bias,
    out_weight,
    out_bias,
    first_gain,
    first_shift,
    up_weight,
    up_bias,
    down_weight,
    down_bias,
    second_gain,
    second_shift,
    cotangent,
):
    tokens = hidden_in.shape[0]
    length = LEN
    blk_rows = min(512, length)
    per_seq = length // blk_rows
    step_count = tokens // length * per_seq
    width_loc = query_weight.shape[1]
    heads_loc = width_loc // HEAD
    row_span = length + blk_rows
    score_scale = 1.0 / math.sqrt(3.0 * HEAD)
    mp_parts = lax.axis_size("mp")
    share_rows = tokens // mp_parts
    my_index = lax.axis_index("mp")

    def project(weight, bias_vec):
        return (
            jnp.dot(hidden_in, weight, preferred_element_type=jnp.float32)
            + bias_vec.astype(jnp.float32)
        ).astype(jnp.bfloat16)

    queries = project(query_weight, query_bias).reshape(tokens, heads_loc, HEAD)
    keys_all = project(key_weight, key_bias).reshape(tokens, heads_loc, HEAD)
    values_all = project(value_weight, value_bias).reshape(tokens, heads_loc, HEAD)
    pos_query = (
        jnp.dot(position_table, query_weight, preferred_element_type=jnp.float32)
        + query_bias.astype(jnp.float32)
    ).astype(jnp.bfloat16)
    pos_key = (
        jnp.dot(position_table, key_weight, preferred_element_type=jnp.float32)
        + key_bias.astype(jnp.float32)
    ).astype(jnp.bfloat16)
    table_rows = position_table.shape[0]
    reversed_at = jnp.concatenate([bucket_of_offset[::-1], bucket_of_offset[:1]])
    one_hot = (reversed_at[:, None] == jnp.arange(table_rows, dtype=jnp.int32)[None, :]).astype(
        jnp.bfloat16
    )
    query_rows = (
        jnp.dot(one_hot, pos_query, preferred_element_type=jnp.float32)
        .astype(jnp.bfloat16)
        .reshape(2 * length, heads_loc, HEAD)
    )
    key_rows = (
        jnp.dot(one_hot, pos_key, preferred_element_type=jnp.float32)
        .astype(jnp.bfloat16)
        .reshape(2 * length, heads_loc, HEAD)
    )

    def score_block(step_at):
        seq_at = step_at // per_seq
        first_row = step_at % per_seq * blk_rows
        seq_base = seq_at * length
        q_blk = take_rows(queries, seq_base + first_row, blk_rows)
        k_seq = take_rows(keys_all, seq_base, length)
        v_seq = take_rows(values_all, seq_base, length)
        live_keys = take_rows(key_mask, seq_base, length)
        pk_blk = take_rows(key_rows, length - first_row - blk_rows, row_span)
        pq_blk = take_rows(query_rows, first_row, row_span)
        content = jnp.einsum("bhd,khd->hbk", q_blk, k_seq, preferred_element_type=jnp.float32)
        to_pos = shear_rows(
            jnp.einsum("bhd,uhd->hbu", q_blk, pk_blk, preferred_element_type=jnp.float32), length
        )
        from_pos = jnp.swapaxes(
            shear_rows(
                jnp.einsum("khd,uhd->hku", k_seq, pq_blk, preferred_element_type=jnp.float32),
                blk_rows,
            ),
            1,
            2,
        )
        masked = jnp.where(
            live_keys[None, None, :] > 0, (content + to_pos + from_pos) * score_scale, MASK_FILL
        )
        return (masked, (q_blk, k_seq, v_seq, pk_blk, pq_blk, seq_base, first_row))

    def forward_block(step_at):
        masked, pieces = score_block(step_at)
        row_max = jnp.max(masked, axis=2, keepdims=True)
        exp_terms = jnp.exp(masked - row_max)
        row_total = jnp.sum(exp_terms, axis=2, keepdims=True)
        prob_low = (exp_terms / row_total).astype(jnp.bfloat16)
        context_blk = jnp.einsum(
            "hbk,khd->bhd", prob_low, pieces[2], preferred_element_type=jnp.float32
        ).astype(jnp.bfloat16)
        return (context_blk, row_max + jnp.log(row_total))

    contexts, log_totals = lax.map(forward_block, jnp.arange(step_count, dtype=jnp.int32))
    context = contexts.reshape(tokens, width_loc)
    attn_share = lax.psum_scatter(
        jnp.dot(
            take_rows(context, jnp.int32(0), share_rows * lax.axis_size("mp")),
            out_weight,
            preferred_element_type=jnp.float32,
        ),
        "mp",
        scatter_dimension=0,
        tiled=True,
    )
    own_rows = take_rows(hidden_in, my_index * share_rows, share_rows).astype(jnp.float32)
    pre_first = attn_share + out_bias.astype(jnp.float32) + own_rows
    normed, first_pull = jax.vjp(
        norm_rows, pre_first, first_gain.astype(jnp.float32), first_shift.astype(jnp.float32)
    )
    normed_low = normed.astype(jnp.bfloat16)
    gathered = lax.all_gather(normed_low, "mp", axis=0, tiled=True)
    inner_pre = jnp.dot(gathered, up_weight, preferred_element_type=jnp.float32) + up_bias.astype(
        jnp.float32
    )
    activated, gelu_pull = jax.vjp(exact_gelu, inner_pre)
    act_low = activated.astype(jnp.bfloat16)
    down_share = lax.psum_scatter(
        jnp.dot(
            take_rows(act_low, jnp.int32(0), share_rows * lax.axis_size("mp")),
            down_weight,
            preferred_element_type=jnp.float32,
        ),
        "mp",
        scatter_dimension=0,
        tiled=True,
    )
    pre_second = down_share + down_bias.astype(jnp.float32) + normed
    result, second_pull = jax.vjp(
        norm_rows, pre_second, second_gain.astype(jnp.float32), second_shift.astype(jnp.float32)
    )
    d_pre_second, second_gain_grad, second_shift_grad = second_pull(cotangent.astype(jnp.float32))
    down_bias_grad = jnp.sum(d_pre_second, axis=0)
    d_down = d_pre_second.astype(jnp.bfloat16)
    part_rows = lax.all_gather(d_down, "mp", axis=0, tiled=True)
    row_count = part_rows.shape[0]
    weight_acc = left_product(take_rows(act_low, jnp.int32(0), row_count), part_rows)
    act_grad = right_product(part_rows, down_weight)
    down_weight_grad, act_grad = (weight_acc, act_grad)
    d_inner = gelu_pull(act_grad)[0].astype(jnp.bfloat16)
    up_bias_grad = jnp.sum(d_inner.astype(jnp.float32), axis=0)
    up_weight_grad = left_product(gathered, d_inner)
    d_normed = (
        lax.psum_scatter(
            right_product(
                take_rows(d_inner, jnp.int32(0), share_rows * lax.axis_size("mp")), up_weight
            ),
            "mp",
            scatter_dimension=0,
            tiled=True,
        )
        + d_pre_second
    )
    d_pre_first, first_gain_grad, first_shift_grad = first_pull(d_normed)
    out_bias_grad = jnp.sum(d_pre_first, axis=0)
    d_attn = d_pre_first.astype(jnp.bfloat16)
    part_rows = lax.all_gather(d_attn, "mp", axis=0, tiled=True)
    row_count = part_rows.shape[0]
    weight_acc = left_product(take_rows(context, jnp.int32(0), row_count), part_rows)
    ctx_grad = right_product(part_rows, out_weight)
    out_weight_grad, ctx_grad = (weight_acc, ctx_grad)
    d_context = ctx_grad.astype(jnp.bfloat16).reshape(tokens, heads_loc, HEAD)

    def backward_block(carry_in, step_at):
        keys_grad, values_grad, pq_grad, pk_grad = carry_in
        masked, pieces = score_block(step_at)
        q_blk, k_seq, v_seq, pk_blk, pq_blk, seq_base, first_row = pieces
        attn_prob = jnp.exp(masked - log_totals[step_at])
        prob_low = attn_prob.astype(jnp.bfloat16)
        dc_blk = take_rows(d_context, seq_base + first_row, blk_rows)
        d_prob = jnp.einsum("bhd,khd->hbk", dc_blk, v_seq, preferred_element_type=jnp.float32)
        row_dot = jnp.sum(d_prob * attn_prob, axis=2, keepdims=True)
        d_score = (attn_prob * (d_prob - row_dot)).astype(jnp.bfloat16)
        d_to = unshear_rows(d_score, row_span).astype(jnp.bfloat16)
        d_from = unshear_rows(jnp.swapaxes(d_score, 1, 2), row_span).astype(jnp.bfloat16)
        q_part = jnp.einsum(
            "hbk,khd->bhd", d_score, k_seq, preferred_element_type=jnp.float32
        ) + jnp.einsum("hbu,uhd->bhd", d_to, pk_blk, preferred_element_type=jnp.float32)
        k_part = jnp.einsum(
            "hbk,bhd->khd", d_score, q_blk, preferred_element_type=jnp.float32
        ) + jnp.einsum("hku,uhd->khd", d_from, pq_blk, preferred_element_type=jnp.float32)
        v_part = jnp.einsum("hbk,bhd->khd", prob_low, dc_blk, preferred_element_type=jnp.float32)
        pk_part = jnp.einsum("hbu,bhd->uhd", d_to, q_blk, preferred_element_type=jnp.float32)
        pq_part = jnp.einsum("hku,khd->uhd", d_from, k_seq, preferred_element_type=jnp.float32)
        keys_grad = add_rows(keys_grad, k_part * score_scale, seq_base)
        values_grad = add_rows(values_grad, v_part, seq_base)
        pk_grad = add_rows(pk_grad, pk_part * score_scale, length - first_row - blk_rows)
        pq_grad = add_rows(pq_grad, pq_part * score_scale, first_row)
        return (
            (keys_grad, values_grad, pq_grad, pk_grad),
            (q_part * score_scale).astype(jnp.bfloat16),
        )

    scan_init = (
        jnp.zeros((tokens, heads_loc, HEAD), jnp.float32),
        jnp.zeros((tokens, heads_loc, HEAD), jnp.float32),
        jnp.zeros((2 * length, heads_loc, HEAD), jnp.float32),
        jnp.zeros((2 * length, heads_loc, HEAD), jnp.float32),
    )
    carry_out, query_grads = lax.scan(
        backward_block, scan_init, jnp.arange(step_count, dtype=jnp.int32)
    )
    keys_grad, values_grad, pq_grad, pk_grad = carry_out
    d_query = query_grads.reshape(tokens, width_loc)
    d_key = keys_grad.astype(jnp.bfloat16).reshape(tokens, width_loc)
    d_value = values_grad.astype(jnp.bfloat16).reshape(tokens, width_loc)
    d_pos_query = left_wide(one_hot, pq_grad.reshape(2 * length, width_loc))
    d_pos_key = left_wide(one_hot, pk_grad.reshape(2 * length, width_loc))
    query_weight_grad = left_product(hidden_in, d_query) + left_wide(position_table, d_pos_query)
    key_weight_grad = left_product(hidden_in, d_key) + left_wide(position_table, d_pos_key)
    value_weight_grad = left_product(hidden_in, d_value)
    query_bias_grad = jnp.sum(d_query.astype(jnp.float32), axis=0) + jnp.sum(d_pos_query, axis=0)
    key_bias_grad = jnp.sum(d_key.astype(jnp.float32), axis=0) + jnp.sum(d_pos_key, axis=0)
    value_bias_grad = jnp.sum(d_value.astype(jnp.float32), axis=0)
    table_grad = right_wide(d_pos_query, query_weight) + right_wide(d_pos_key, key_weight)
    start_at = jnp.int32(0)
    input_grad = (
        lax.psum_scatter(
            (
                right_product(
                    take_rows(d_query, start_at, lax.axis_size("mp") * share_rows), query_weight
                )
                + right_product(
                    take_rows(d_key, start_at, lax.axis_size("mp") * share_rows), key_weight
                )
                + right_product(
                    take_rows(d_value, start_at, lax.axis_size("mp") * share_rows), value_weight
                )
            ).astype(jnp.bfloat16),
            "mp",
            scatter_dimension=0,
            tiled=True,
        ).astype(jnp.float32)
        + d_pre_first
    )
    (
        query_weight_grad,
        query_bias_grad,
        key_weight_grad,
        key_bias_grad,
        value_weight_grad,
        value_bias_grad,
        out_weight_grad,
        up_weight_grad,
        up_bias_grad,
        down_weight_grad,
    ) = (
        lax.psum(query_weight_grad.astype(jnp.bfloat16), "dp").astype(jnp.float32),
        lax.psum(query_bias_grad.astype(jnp.bfloat16), "dp").astype(jnp.float32),
        lax.psum(key_weight_grad.astype(jnp.bfloat16), "dp").astype(jnp.float32),
        lax.psum(key_bias_grad.astype(jnp.bfloat16), "dp").astype(jnp.float32),
        lax.psum(value_weight_grad.astype(jnp.bfloat16), "dp").astype(jnp.float32),
        lax.psum(value_bias_grad.astype(jnp.bfloat16), "dp").astype(jnp.float32),
        lax.psum(out_weight_grad.astype(jnp.bfloat16), "dp").astype(jnp.float32),
        lax.psum(up_weight_grad.astype(jnp.bfloat16), "dp").astype(jnp.float32),
        lax.psum(up_bias_grad.astype(jnp.bfloat16), "dp").astype(jnp.float32),
        lax.psum(down_weight_grad.astype(jnp.bfloat16), "dp").astype(jnp.float32),
    )
    (
        table_grad,
        out_bias_grad,
        first_gain_grad,
        first_shift_grad,
        down_bias_grad,
        second_gain_grad,
        second_shift_grad,
    ) = lax.psum(
        (
            table_grad,
            out_bias_grad,
            first_gain_grad,
            first_shift_grad,
            down_bias_grad,
            second_gain_grad,
            second_shift_grad,
        ),
        ("dp", "mp"),
    )
    return (
        result.astype(jnp.bfloat16),
        input_grad,
        table_grad,
        query_weight_grad,
        query_bias_grad,
        key_weight_grad,
        key_bias_grad,
        value_weight_grad,
        value_bias_grad,
        out_weight_grad,
        out_bias_grad,
        first_gain_grad,
        first_shift_grad,
        up_weight_grad,
        up_bias_grad,
        down_weight_grad,
        down_bias_grad,
        second_gain_grad,
        second_shift_grad,
    )


def solution(mesh):
    return jax.shard_map(
        on_device,
        mesh=mesh,
        in_specs=(
            P("dp", None),
            P("dp"),
            P(),
            P(),
            P(None, "mp"),
            P("mp"),
            P(None, "mp"),
            P("mp"),
            P(None, "mp"),
            P("mp"),
            P("mp", None),
            P(),
            P(),
            P(),
            P(None, "mp"),
            P("mp"),
            P("mp", None),
            P(),
            P(),
            P(),
            P(("dp", "mp"), None),
        ),
        out_specs=(
            P(("dp", "mp"), None),
            P(("dp", "mp"), None),
            P(),
            P(None, "mp"),
            P("mp"),
            P(None, "mp"),
            P("mp"),
            P(None, "mp"),
            P("mp"),
            P("mp", None),
            P(),
            P(),
            P(),
            P(None, "mp"),
            P("mp"),
            P("mp", None),
            P(),
            P(),
            P(),
        ),
        check_vma=False,
    )
```

profile of v0, /device:TPU:0, one launch (start us, length us, event | category | flops | bytes accessed | tf_op | source)
XLA Modules:
  0.0 4190.8 jit_solution(18441991590339944222)
XLA Ops:
  29.7 1090.8 %while.41 = (s32[]{:T(128)}, bf16[2,512,4,64]{1,3,2,0:T(8,128)(2,1)}, f32[2,4,512,1]{2,1,3,0:T(4,128)}, s32[1024]{0:T(1024)}, s32[2]{0:T(128)}, /*index=5*/bf16[...) while((s32[]{:T(128)}, ...), condition=%wide.region_3.4_spmd, body=%wide.region_0.3_spmd.sunk | while | flops 1852295680 | bytes 2133026304 | solution.py:191
  282.8 16.9 pad_select_fusion.68
  308.6 19.2 pad_select_fusion.69
  327.8 21.3 slice.562
  351.9 19.2 pad_select_fusion.70
  379.2 19.0 pad_select_fusion.71
  406.4 19.2 pad_select_fusion.72
  433.6 19.1 pad_select_fusion.73
  460.5 19.1 pad_select_fusion.74
  487.2 19.1 pad_select_fusion.75
  513.3 19.1 pad_select_fusion.76
  824.5 16.9 pad_select_fusion.68
  850.3 19.2 pad_select_fusion.69
  869.5 21.3 slice.562
  893.7 19.2 pad_select_fusion.70
  921.0 19.0 pad_select_fusion.71
  948.1 19.4 pad_select_fusion.72
  975.6 19.1 pad_select_fusion.73
  1002.5 19.1 pad_select_fusion.74
  1029.2 19.1 pad_select_fusion.75
  1055.2 19.1 pad_select_fusion.76
  1127.0 79.5 %reduce-scatter.5.cloned.1.call-done = f32[256,1024]{1,0:T(8,128)} async-done(((f32[1024,1024]{1,0:T(8,128)}), f32[256,1024]{1,0:T(8,128)}) %reduce-scatter.5.cloned.1.call-update) | async-done | bytes 1048592 | tf_op jit(solution)/shard_map/reduce_scatter | solution.py:193
  1210.2 46.5 %all-gather.4.cloned.1.call-done = bf16[1024,1024]{1,0:T(8,128)(2,1)} async-done(((bf16[256,1024]{1,0:T(8,128)(2,1)}), bf16[1024,1024]{1,0:T(8,128)(2,1)}) %all-gather.4.cloned.1.call-update) | async-done | bytes 2097168 | tf_op jit(solution)/shard_map/all_gather | solution.py:209
  1276.7 75.5 %reduce-scatter.7.cloned.1.call-done = f32[256,1024]{1,0:T(8,128)} async-done(((f32[1024,1024]{1,0:T(8,128)}), f32[256,1024]{1,0:T(8,128)}) %reduce-scatter.7.cloned.1.call-update) | async-done | bytes 1048592 | tf_op jit(solution)/shard_map/reduce_scatter | solution.py:215
  1361.7 46.3 %all-gather.6.cloned.1.call-done = bf16[1024,1024]{1,0:T(8,128)(2,1)} async-done(((bf16[256,1024]{1,0:T(8,128)(2,1)}), bf16[1024,1024]{1,0:T(8,128)(2,1)}) %all-gather.6.cloned.1.call-update) | async-done | bytes 2097168 | tf_op jit(solution)/shard_map/all_gather | solution.py:232
  1422.6 75.6 %reduce-scatter.9.cloned.1.call-done = f32[256,1024]{1,0:T(8,128)} async-done(((f32[1024,1024]{1,0:T(8,128)}), f32[256,1024]{1,0:T(8,128)}) %reduce-scatter.9.cloned.1.call-update) | async-done | bytes 1048592 | tf_op jit(solution)/shard_map/reduce_scatter | solution.py:241
  1514.6 36.6 all-gather.8.cloned.1.call-done
  1558.8 2307.7 %while.42 = (s32[]{:T(128)}, f32[1024,4,64]{0,2,1:T(8,128)}, f32[1024,4,64]{0,2,1:T(8,128)}, f32[2048,4,64]{0,2,1:T(8,128)}, f32[2048,4,64]{0,2,1:T(8,128)}, /*i...) while((s32[]{:T(128)}, f32[1024,4,64]{0,2,1:T(8,128)}, ...), condition=%wide.region_17.18_spmd.clone, body=%wide.region_15.17_spmd.clone.sunk | while | flops 5394620928 | bytes 4834737664 | solution.py:297
  1820.0 16.9 pad_select_fusion.85
  1845.8 19.2 pad_select_fusion.86
  1865.0 21.3 slice.583
  1889.2 19.2 pad_select_fusion.87
  1916.4 19.2 pad_select_fusion.88
  1943.7 19.0 pad_select_fusion.89
  1970.8 19.1 pad_select_fusion.90
  1997.7 19.1 pad_select_fusion.91
  2024.3 19.1 pad_select_fusion.92
  2050.4 19.1 pad_select_fusion.93
  2374.3 17.0 slice_select_fusion.43
  2560.8 16.9 pad_add_fusion.41
  2586.8 19.5 pad_add_fusion.42
  2606.3 19.0 slice_select_fusion.50
  2630.5 19.3 pad_add_fusion.43
  2649.8 19.0 slice_select_fusion.51
  2969.5 16.9 pad_select_fusion.85
  2995.3 19.2 pad_select_fusion.86
  3014.4 21.3 slice.583
  3038.6 19.2 pad_select_fusion.87
  3065.9 19.2 pad_select_fusion.88
  3093.2 19.0 pad_select_fusion.89
  3120.3 19.1 pad_select_fusion.90
  3147.2 19.1 pad_select_fusion.91
  3173.8 19.1 pad_select_fusion.92
  3199.9 19.1 pad_select_fusion.93
  3523.8 17.0 slice_select_fusion.43
  3710.3 16.9 pad_add_fusion.41
  3736.3 19.5 pad_add_fusion.42
  3755.8 19.0 slice_select_fusion.50
  3780.0 19.3 pad_add_fusion.43
  3799.3 19.0 slice_select_fusion.51
  3902.2 40.6 all-reduce.59
  3960.1 34.5 all-reduce.67.cloned.1.call-done
  4011.7 29.8 reduce-scatter.11.cloned.1.call-done
  4043.7 137.1 %all-reduce.65.cloned.1.call-done = f32[512,1024]{1,0:T(8,128)} async-done(((f32[512,1024]{1,0:T(8,128)}), f32[512,1024]{1,0:T(8,128)}) %all-reduce.65.cloned.1.call-update) | async-done | bytes 2097168 | tf_op jit(solution)/shard_map/psum | solution.py:364
  (848 shorter events, 2556.5 us)
Async XLA Ops:
  7.2 1249.6 %copy-start = (bf16[1024,1024]{1,0:T(8,128)(2,1)S(1)}, bf16[1024,1024]{1,0:T(8,128)(2,1)}, u32[]{:S(2)}) copy-start(bf16[1024,1024]{1,0:T(8,128)(2,1)} %param.39) | copy-start | bytes 6291460
  7.2 17.9 copy-start.128
  7.2 1199.3 %reduce-scatter.5.cloned.1.call-start = ((), (), s32[]{:S(2)}) async-start(), calls=%async_computation.4 | async-start | bytes 5242880 | tf_op jit(solution)/shard_map/reduce_scatter | solution.py:193
  11.5 18.2 copy-start.115
  30.2 30.8 copy-start.22
  327.7 24.2 copy-start.4
  327.8 24.2 copy-start.103
  571.9 30.8 copy-start.22
  869.5 24.2 copy-start.4
  869.5 24.2 copy-start.103
  1120.5 89.6 %copy-start.120 = (bf16[1024]{0:T(1024)(128)(2,1)S(1)}, bf16[1024]{0:T(1024)(128)(2,1)}, u32[]{:S(2)}) copy-start(bf16[1024]{0:T(1024)(128)(2,1)} %param.40) | copy-start | bytes 6148
  1126.9 129.9 %all-gather.4.cloned.1.call-start = ((), (), s32[]{:S(2)}) async-start(), calls=%async_computation.5 | async-start | bytes 2621440 | tf_op jit(solution)/shard_map/all_gather | solution.py:209
  1210.1 142.1 %reduce-scatter.7.cloned.1.call-start = ((), (), s32[]{:S(2)}) async-start(), calls=%async_computation.6 | async-start | bytes 5242880 | tf_op jit(solution)/shard_map/reduce_scatter | solution.py:215
  1276.6 131.4 %all-gather.6.cloned.1.call-start = ((), (), s32[]{:S(2)}) async-start(), calls=%async_computation.7 | async-start | bytes 2621440 | tf_op jit(solution)/shard_map/all_gather | solution.py:232
  1361.3 136.9 %reduce-scatter.9.cloned.1.call-start = ((), (), s32[]{:S(2)}) async-start(), calls=%async_computation.8 | async-start | bytes 5242880 | tf_op jit(solution)/shard_map/reduce_scatter | solution.py:241
  1422.6 128.6 %all-gather.8.cloned.1.call-start = ((), (), s32[]{:S(2)}) async-start(), calls=%async_computation.9 | async-start | bytes 2621440 | tf_op jit(solution)/shard_map/all_gather | solution.py:254
  1504.6 2490.0 %all-reduce.67.cloned.1.call-start = ((), (), s32[]{:S(2)}) async-start(), calls=%async_computation.12 | async-start | bytes 12582912 | tf_op jit(solution)/shard_map/psum | solution.py:345
  1510.8 40.4 copy-start.56
  1559.3 31.2 copy-start.24
  1564.5 26.0 copy-start.78
  1566.3 208.2 %copy-start.75 = (pred[512]{0:T(512)(128)(4,1)}, pred[512]{0:T(512)(128)(4,1)S(1)}, u32[]{:S(2)}) copy-start(pred[512]{0:T(512)(128)(4,1)S(1)} %get-tuple-element.1112) | copy-start | bytes 1540 | tf_op jit(solution)/shard_map/while
  1566.3 157.7 %copy-start.88 = (pred[512]{0:T(512)(128)(4,1)}, pred[512]{0:T(512)(128)(4,1)S(1)}, u32[]{:S(2)}) copy-start(pred[512]{0:T(512)(128)(4,1)S(1)} %get-tuple-element.1110) | copy-start | bytes 1540 | tf_op jit(solution)/shard_map/while
  1566.3 184.3 %copy-start.90 = (pred[512]{0:T(512)(128)(4,1)}, pred[512]{0:T(512)(128)(4,1)S(1)}, u32[]{:S(2)}) copy-start(pred[512]{0:T(512)(128)(4,1)S(1)} %get-tuple-element.1111) | copy-start | bytes 1540 | tf_op jit(solution)/shard_map/while
  1566.3 104.2 %copy-start.84 = (pred[512]{0:T(512)(128)(4,1)}, pred[512]{0:T(512)(128)(4,1)S(1)}, u32[]{:S(2)}) copy-start(pred[512]{0:T(512)(128)(4,1)S(1)} %get-tuple-element.1108) | copy-start | bytes 1540 | tf_op jit(solution)/shard_map/while
  1566.3 131.0 %copy-start.86 = (pred[512]{0:T(512)(128)(4,1)}, pred[512]{0:T(512)(128)(4,1)S(1)}, u32[]{:S(2)}) copy-start(pred[512]{0:T(512)(128)(4,1)S(1)} %get-tuple-element.1109) | copy-start | bytes 1540 | tf_op jit(solution)/shard_map/while
  1566.4 50.9 %copy-start.80 = (pred[512]{0:T(512)(128)(4,1)}, pred[512]{0:T(512)(128)(4,1)S(1)}, u32[]{:S(2)}) copy-start(pred[512]{0:T(512)(128)(4,1)S(1)} %get-tuple-element.1106) | copy-start | bytes 1540 | tf_op jit(solution)/shard_map/while
  1566.4 77.5 %copy-start.82 = (pred[512]{0:T(512)(128)(4,1)}, pred[512]{0:T(512)(128)(4,1)S(1)}, u32[]{:S(2)}) copy-start(pred[512]{0:T(512)(128)(4,1)S(1)} %get-tuple-element.1107) | copy-start | bytes 1540 | tf_op jit(solution)/shard_map/while
  1865.0 24.2 copy-start.8
  1865.0 24.2 copy-start.63
  2391.3 25.0 copy-start.58
  2424.9 24.7 copy-start.72
  2458.3 25.0 copy-start.70
  2492.2 25.1 copy-start.68
  2526.4 25.2 copy-start.66
  2586.8 19.5 copy-start.62
  2606.3 24.2 copy-start.5
  2630.5 19.3 copy-start.60
  2649.8 24.2 copy-start.6
  2708.7 31.2 copy-start.24
  2713.9 26.0 copy-start.78
  2715.7 208.2 %copy-start.75 = (pred[512]{0:T(512)(128)(4,1)}, pred[512]{0:T(512)(128)(4,1)S(1)}, u32[]{:S(2)}) copy-start(pred[512]{0:T(512)(128)(4,1)S(1)} %get-tuple-element.1112) | copy-start | bytes 1540 | tf_op jit(solution)/shard_map/while
  2715.8 157.7 %copy-start.88 = (pred[512]{0:T(512)(128)(4,1)}, pred[512]{0:T(512)(128)(4,1)S(1)}, u32[]{:S(2)}) copy-start(pred[512]{0:T(512)(128)(4,1)S(1)} %get-tuple-element.1110) | copy-start | bytes 1540 | tf_op jit(solution)/shard_map/while
  2715.8 184.3 %copy-start.90 = (pred[512]{0:T(512)(128)(4,1)}, pred[512]{0:T(512)(128)(4,1)S(1)}, u32[]{:S(2)}) copy-start(pred[512]{0:T(512)(128)(4,1)S(1)} %get-tuple-element.1111) | copy-start | bytes 1540 | tf_op jit(solution)/shard_map/while
  2715.8 104.2 %copy-start.84 = (pred[512]{0:T(512)(128)(4,1)}, pred[512]{0:T(512)(128)(4,1)S(1)}, u32[]{:S(2)}) copy-start(pred[512]{0:T(512)(128)(4,1)S(1)} %get-tuple-element.1108) | copy-start | bytes 1540 | tf_op jit(solution)/shard_map/while
  2715.8 131.0 %copy-start.86 = (pred[512]{0:T(512)(128)(4,1)}, pred[512]{0:T(512)(128)(4,1)S(1)}, u32[]{:S(2)}) copy-start(pred[512]{0:T(512)(128)(4,1)S(1)} %get-tuple-element.1109) | copy-start | bytes 1540 | tf_op jit(solution)/shard_map/while
  2715.9 50.9 %copy-start.80 = (pred[512]{0:T(512)(128)(4,1)}, pred[512]{0:T(512)(128)(4,1)S(1)}, u32[]{:S(2)}) copy-start(pred[512]{0:T(512)(128)(4,1)S(1)} %get-tuple-element.1106) | copy-start | bytes 1540 | tf_op jit(solution)/shard_map/while
  2715.9 77.5 %copy-start.82 = (pred[512]{0:T(512)(128)(4,1)}, pred[512]{0:T(512)(128)(4,1)S(1)}, u32[]{:S(2)}) copy-start(pred[512]{0:T(512)(128)(4,1)S(1)} %get-tuple-element.1107) | copy-start | bytes 1540 | tf_op jit(solution)/shard_map/while
  3014.4 24.2 copy-start.8
  3014.4 24.2 copy-start.63
  3540.8 25.0 copy-start.58
  3574.4 24.7 copy-start.72
  3607.8 25.0 copy-start.70
  3641.7 25.1 copy-start.68
  3675.9 25.2 copy-start.66
  3736.3 19.5 copy-start.62
  3755.8 24.2 copy-start.5
  3780.0 19.3 copy-start.60
  3799.3 24.2 copy-start.6
  3889.2 152.4 %reduce-scatter.11.cloned.1.call-start = ((), (), s32[]{:S(2)}) async-start(), calls=%async_computation.10 | async-start | bytes 2621440 | tf_op jit(solution)/shard_map/reduce_scatter | solution.py:315
  3894.2 50.1 %copy-start.124 = (bf16[1024]{0:T(1024)(128)(2,1)S(1)}, bf16[1024]{0:T(1024)(128)(2,1)}, u32[]{:S(2)}) copy-start(bf16[1024]{0:T(1024)(128)(2,1)} %get-tuple-element.836) | copy-start | bytes 6148
  3894.2 286.6 %all-reduce.65.cloned.1.call-start = ((), (), s32[]{:S(2)}) async-start(), calls=%async_computation.11 | async-start | bytes 4194304 | tf_op jit(solution)/shard_map/psum | solution.py:364
  3902.1 139.4 %copy-start.40 = (f32[256,1024]{1,0:T(8,128)S(1)}, f32[256,1024]{1,0:T(8,128)}, u32[]{:S(2)}) copy-start(f32[256,1024]{1,0:T(8,128)} %copy-done.39) | copy-start | bytes 3145732
  3902.1 139.4 %copy-start.114 = (f32[256]{0:T(256)S(1)}, f32[256]{0:T(256)}, u32[]{:S(2)}) copy-start(f32[256]{0:T(256)} %copy-done.113) | copy-start | bytes 3076
  3996.8 187.2 %copy-start.1 = (bf16[1024,1024]{1,0:T(8,128)(2,1)S(1)}, bf16[1024,1024]{1,0:T(8,128)(2,1)}, u32[]{:S(2)}) copy-start(bf16[1024,1024]{1,0:T(8,128)(2,1)} %param.39) | copy-start | bytes 6291460
  (190 other events, 1793.9 us)
Sparse Core Ops, SparseCore 0:
  1127.0 79.4 reduce-scatter.4
  1210.3 46.4 all-gather.3
  1276.7 75.4 reduce-scatter.6
  1361.5 46.4 all-gather.5
  1422.7 75.4 reduce-scatter.8
  1504.7 46.4 all-gather.7
  3889.3 105.2 all-reduce.66
  3997.5 44.0 reduce-scatter.10
  4047.7 133.0 all-reduce.64
where the time goes:
time: 4200 us; the launch traced here: 4190 us
  other arithmetic  2260 us (54%)
  local copies, waits for them, and re-layouts  998 us (24%)
  waiting for transfers between devices  562 us (13%)
  matrix products  271 us (6%)
  blocking collectives  54.1 us (1%)
    select_n x106, other arithmetic, shear_rows(): current = jnp.where(chosen, moved, current)  1550 us
    slice x102, local copies, waits for them, and re-layouts, shear_rows(): moved = jnp.concatenate([current[..., step_size:], filler], axis=-1)  810 us
    add_any x34, other arithmetic, shear_rows(): moved = jnp.concatenate([current[..., step_size:], filler], axis=-1)  531 us
    while x348, local copies, waits for them, and re-layouts  153 us
    psum x1, waiting for transfers between devices, on_device(): lax.psum((table_grad, out_bias_grad, first_gain_grad, first_shift_grad, d...  137 us
  transfers between devices with their start and end apart: 9, of which 9 were waited for; matrix products, arithmetic and copies ran while one was open for 1% of the time, Pallas kernels for 0%

commit v1 on v0

v1 whole, which is shorter than its diff:
```python
import math

import jax
import jax.numpy as jnp
from jax import lax
from jax.experimental import pallas as pl
from jax.experimental.pallas import tpu as pltpu
from jax.sharding import PartitionSpec as P

HEAD = 64
LEN = 1024


NORM_EPS = 1e-07
MASK_FILL = -1000000000.0


def norm_rows(values, gain_vec, shift_vec):
    row_mean = jnp.mean(values, axis=-1, keepdims=True)
    centered = values - row_mean
    row_var = jnp.mean(centered * centered, axis=-1, keepdims=True)
    return centered * lax.rsqrt(row_var + NORM_EPS) * gain_vec + shift_vec


def exact_gelu(values):
    return jax.nn.gelu(values, approximate=False)


def take_rows(values, start_at, row_count):
    return lax.dynamic_slice_in_dim(values, start_at, row_count, 0)


def add_rows(total_acc, part_rows, start_at):
    current = take_rows(total_acc, start_at, part_rows.shape[0])
    return lax.dynamic_update_slice_in_dim(total_acc, current + part_rows, start_at, 0)


def left_product(left_arr, right_arr):
    return lax.dot_general(
        left_arr, right_arr, (((0,), (0,)), ((), ())), preferred_element_type=jnp.float32
    )


def right_product(left_arr, right_arr):
    return lax.dot_general(
        left_arr, right_arr, (((1,), (1,)), ((), ())), preferred_element_type=jnp.float32
    )


def split_wide(values):
    upper_part = values.astype(jnp.bfloat16)
    lower_part = (values - upper_part.astype(jnp.float32)).astype(jnp.bfloat16)
    return (upper_part, lower_part)


def left_wide(narrow, wide_arr):
    upper_part, lower_part = split_wide(wide_arr)
    return left_product(narrow, upper_part) + left_product(narrow, lower_part)


def right_wide(wide_arr, narrow):
    upper_part, lower_part = split_wide(wide_arr)
    return right_product(upper_part, narrow) + right_product(lower_part, narrow)


NT=(((1,),(1,)),((),()))
NN=(((1,),(0,)),((),()))
TN=(((0,),(0,)),((),()))
def dot(a,b,dims):
    return lax.dot_general(a,b,dims,preferred_element_type=jnp.float32)
BLK=128
SCALE=1.0/math.sqrt(3.0*HEAD)

def half_of(x, half):
    lane=lax.broadcasted_iota(jnp.int32,(1,2*HEAD),1)
    return jnp.where((lane>=HEAD) if half else (lane<HEAD), x, jnp.zeros_like(x))

def eye(n):
    r=lax.broadcasted_iota(jnp.int32,(n,n),0); c=lax.broadcasted_iota(jnp.int32,(n,n),1)
    return (r==c).astype(jnp.float32).astype(jnp.bfloat16)

def shear(x):
    return pltpu.roll(x,0,1,stride=1,stride_axis=0)[:,BLK:]

def unshear(x, length):
    w=length+BLK
    x=jnp.concatenate([jnp.zeros((x.shape[0],BLK),x.dtype),x],axis=1)
    return pltpu.roll(x,0,1,stride=w-1,stride_axis=0)

def fwd_kernel(q_ref,k_ref,v_ref,kr_ref,qr_ref,mask_ref,p_ref,ctx_ref,f_scr):
    length=q_ref.shape[0]; nb=length//BLK; span=length+BLK
    def jb(b,_):
        j0=pl.multiple_of(b*BLK,BLK)
        slab=qr_ref[pl.ds(pl.multiple_of(length-BLK-j0,BLK),span),:]
        kb=k_ref[pl.ds(j0,BLK),:]
        for half in (0,1):
            g=dot(half_of(kb,half),slab,NT)
            f_scr[half,pl.ds(j0,BLK),:]=shear(g).astype(jnp.bfloat16)
        return 0
    lax.fori_loop(0,nb,jb,0)
    ident=eye(BLK)
    live=mask_ref[...]>0
    lane=lax.broadcasted_iota(jnp.int32,(1,2*HEAD),1)
    def ib(b,_):
        i0=pl.multiple_of(b*BLK,BLK)
        slab=kr_ref[pl.ds(pl.multiple_of(length-BLK-i0,BLK),span),:]
        qb=q_ref[pl.ds(i0,BLK),:]
        cs=[]
        for half in (0,1):
            qm=half_of(qb,half)
            t=shear(dot(qm,slab,NT))
            lhs=jnp.concatenate([ident,qm],axis=1)
            rhs=jnp.concatenate([f_scr[half,:,pl.ds(i0,BLK)],k_ref[...]],axis=1)
            s=(dot(lhs,rhs,NT)+t)*SCALE
            s=jnp.where(live,s,MASK_FILL)
            e=jnp.exp(s-jnp.max(s,axis=1,keepdims=True))
            p=(e*(1.0/jnp.sum(e,axis=1,keepdims=True))).astype(jnp.bfloat16)
            p_ref[half,pl.ds(i0,BLK),:]=p
            cs.append(dot(p,v_ref[...],NN))
        ctx_ref[pl.ds(i0,BLK),:]=jnp.where(lane<HEAD,cs[0],cs[1]).astype(jnp.bfloat16)
        return 0
    lax.fori_loop(0,nb,ib,0)

def attn_fwd(q,k,v,kr,qr,mask):
    length,width=q.shape
    pairs=width//(2*HEAD)
    col=pl.BlockSpec((length,2*HEAD),lambda g:(0,g))
    rows=pl.BlockSpec((2*length,2*HEAD),lambda g:(0,g))
    return pl.pallas_call(fwd_kernel,grid=(pairs,),
        in_specs=[col,col,col,rows,rows,pl.BlockSpec((1,length),lambda g:(0,0))],
        out_specs=[pl.BlockSpec((2,length,length),lambda g:(g,0,0)),col],
        out_shape=[jax.ShapeDtypeStruct((2*pairs,length,length),jnp.bfloat16),jax.ShapeDtypeStruct((length,width),jnp.bfloat16)],
        scratch_shapes=[pltpu.VMEM((2,length,length),jnp.bfloat16)],
        compiler_params=pltpu.CompilerParams(vmem_limit_bytes=56*2**20))(q,k,v,kr,qr,mask)

def flip(n):
    r=lax.broadcasted_iota(jnp.int32,(n,n),0); c=lax.broadcasted_iota(jnp.int32,(n,n),1)
    return (r+c==n-1).astype(jnp.float32).astype(jnp.bfloat16)

def spread(x, base):
    x=jnp.concatenate([x,jnp.zeros((x.shape[0],BLK),x.dtype)],axis=1)
    return pltpu.roll(x,base,1,stride=1,stride_axis=0)

def bwd_kernel(q_ref,k_ref,v_ref,kr_ref,qr_ref,p_ref,dc_ref,dq_ref,dk_ref,dv_ref,dkr_ref,dqr_ref,ds_scr,qrev_scr,dvt_scr,dkrt_scr,dqrt_scr):
    length=q_ref.shape[0]; nb=length//BLK; span=length+BLK
    lane=lax.broadcasted_iota(jnp.int32,(1,2*HEAD),1)
    ident=eye(BLK); rev=flip(BLK)
    bf=jnp.bfloat16
    dvt_scr[...]=jnp.zeros_like(dvt_scr)
    dkrt_scr[...]=jnp.zeros_like(dkrt_scr)
    dqrt_scr[...]=jnp.zeros_like(dqrt_scr)
    def ib(b,_):
        i0=pl.multiple_of(b*BLK,BLK)
        u0=pl.multiple_of(length-BLK-i0,BLK)
        slab=kr_ref[pl.ds(u0,span),:]
        qb=dot(rev,q_ref[pl.ds(i0,BLK),:],NN).astype(bf)
        qrev_scr[pl.ds(u0,BLK),:]=qb
        dcb=dc_ref[pl.ds(i0,BLK),:]
        dcr=dot(rev,dcb,NN).astype(bf)
        outs=[]; dvt=0; dkrt=0
        for half in (0,1):
            qm=half_of(qb,half)
            p=p_ref[half,pl.ds(i0,BLK),:]
            dp=dot(half_of(dcr,half),v_ref[...],NT)
            pr=dot(rev,p,NN)
            pd=pr*dp
            ds=pd-pr*jnp.sum(pd,axis=1,keepdims=True)
            dsl=ds.astype(bf)
            ds_scr[half,pl.ds(u0,BLK),:]=dsl
            dto=spread(ds,1).astype(bf)
            outs.append(dot(dsl,k_ref[...],NN)+dot(dto,slab,NN))
            dvt=dvt+dot(half_of(dcb,half),p,TN)
            dkrt=dkrt+dot(qm,dto,TN)
        dqb=(jnp.where(lane<HEAD,outs[0],outs[1])*SCALE).astype(bf)
        dq_ref[pl.ds(i0,BLK),:]=dot(rev,dqb,NN).astype(bf)
        dvt_scr[...]+=dvt
        dkrt_scr[:,pl.ds(u0,span)]+=dkrt
        return 0
    lax.fori_loop(0,nb,ib,0)
    def jb(b,_):
        j0=pl.multiple_of(b*BLK,BLK)
        slab=qr_ref[pl.ds(j0,span),:]
        kb=k_ref[pl.ds(j0,BLK),:]
        outs=[]; dqrt=0
        for half in (0,1):
            km=half_of(kb,half)
            dst=dot(ident,ds_scr[half,:,pl.ds(j0,BLK)],NT)
            dfrom=spread(dst,0).astype(bf)
            outs.append(dot(dst.astype(bf),qrev_scr[...],NN)+dot(dfrom,slab,NN))
            dqrt=dqrt+dot(km,dfrom,TN)
        dk_ref[pl.ds(j0,BLK),:]=(jnp.where(lane<HEAD,outs[0],outs[1])*SCALE).astype(bf)
        dqrt_scr[:,pl.ds(j0,span)]+=dqrt
        return 0
    lax.fori_loop(0,nb,jb,0)
    dv_ref[...]=dvt_scr[...].T.astype(bf)
    dkr_ref[...]=dkrt_scr[...]*SCALE
    dqr_ref[...]=dqrt_scr[...]*SCALE

def attn_bwd(q,k,v,kr,qr,p,dc):
    length,width=q.shape
    pairs=width//(2*HEAD)
    col=pl.BlockSpec((length,2*HEAD),lambda g:(0,g))
    rows=pl.BlockSpec((2*length,2*HEAD),lambda g:(0,g))
    rowst=pl.BlockSpec((2*HEAD,2*length),lambda g:(g,0))
    f32=jnp.float32
    cs=jax.ShapeDtypeStruct((length,width),jnp.bfloat16)
    return pl.pallas_call(bwd_kernel,grid=(pairs,),
        in_specs=[col,col,col,rows,rows,pl.BlockSpec((2,length,length),lambda g:(g,0,0)),col],
        out_specs=[col,col,col,rowst,rowst],
        out_shape=[cs,cs,cs,jax.ShapeDtypeStruct((width,2*length),f32),jax.ShapeDtypeStruct((width,2*length),f32)],
        scratch_shapes=[pltpu.VMEM((2,length,length),jnp.bfloat16),pltpu.VMEM((length,2*HEAD),jnp.bfloat16),pltpu.VMEM((2*HEAD,length),f32),pltpu.VMEM((2*HEAD,2*length),f32),pltpu.VMEM((2*HEAD,2*length),f32)],
        compiler_params=pltpu.CompilerParams(vmem_limit_bytes=60*2**20))(q,k,v,kr,qr,p,dc)


def on_device(
    hidden_in,
    key_mask,
    bucket_of_offset,
    position_table,
    query_weight,
    query_bias,
    key_weight,
    key_bias,
    value_weight,
    value_bias,
    out_weight,
    out_bias,
    first_gain,
    first_shift,
    up_weight,
    up_bias,
    down_weight,
    down_bias,
    second_gain,
    second_shift,
    cotangent,
):
    tokens = hidden_in.shape[0]
    length = LEN
    width_loc = query_weight.shape[1]
    mp_parts = lax.axis_size("mp")
    share_rows = tokens // mp_parts
    my_index = lax.axis_index("mp")

    def project(weight, bias_vec):
        return (
            jnp.dot(hidden_in, weight, preferred_element_type=jnp.float32)
            + bias_vec.astype(jnp.float32)
        ).astype(jnp.bfloat16)

    queries = project(query_weight, query_bias)
    keys_all = project(key_weight, key_bias)
    values_all = project(value_weight, value_bias)
    pos_query = (
        jnp.dot(position_table, query_weight, preferred_element_type=jnp.float32)
        + query_bias.astype(jnp.float32)
    ).astype(jnp.bfloat16)
    pos_key = (
        jnp.dot(position_table, key_weight, preferred_element_type=jnp.float32)
        + key_bias.astype(jnp.float32)
    ).astype(jnp.bfloat16)
    table_rows = position_table.shape[0]
    row_ids = jnp.arange(table_rows, dtype=jnp.int32)[None, :]
    falling = jnp.concatenate([bucket_of_offset[:1], bucket_of_offset[::-1]])
    rising = jnp.concatenate([bucket_of_offset, bucket_of_offset[:1]])
    hot_falling = (falling[:, None] == row_ids).astype(jnp.bfloat16)
    hot_rising = (rising[:, None] == row_ids).astype(jnp.bfloat16)

    def expand(one_hot, rows):
        return jnp.dot(one_hot, rows, preferred_element_type=jnp.float32).astype(jnp.bfloat16)

    key_rows = expand(hot_falling, pos_key)
    query_rows = expand(hot_falling, pos_query)
    query_rows_up = expand(hot_rising, pos_query)
    probs, context = attn_fwd(
        queries, keys_all, values_all, key_rows, query_rows, key_mask.reshape(1, length)
    )
    attn_share = lax.psum_scatter(
        jnp.dot(
            take_rows(context, jnp.int32(0), share_rows * lax.axis_size("mp")),
            out_weight,
            preferred_element_type=jnp.float32,
        ).astype(jnp.bfloat16),
        "mp",
        scatter_dimension=0,
        tiled=True,
    ).astype(jnp.float32)
    own_rows = take_rows(hidden_in, my_index * share_rows, share_rows).astype(jnp.float32)
    pre_first = attn_share + out_bias.astype(jnp.float32) + own_rows
    normed, first_pull = jax.vjp(
        norm_rows, pre_first, first_gain.astype(jnp.float32), first_shift.astype(jnp.float32)
    )
    normed_low = normed.astype(jnp.bfloat16)
    gathered = lax.all_gather(normed_low, "mp", axis=0, tiled=True)
    inner_pre = jnp.dot(gathered, up_weight, preferred_element_type=jnp.float32) + up_bias.astype(
        jnp.float32
    )
    activated, gelu_pull = jax.vjp(exact_gelu, inner_pre)
    act_low = activated.astype(jnp.bfloat16)
    down_share = lax.psum_scatter(
        jnp.dot(
            take_rows(act_low, jnp.int32(0), share_rows * lax.axis_size("mp")),
            down_weight,
            preferred_element_type=jnp.float32,
        ).astype(jnp.bfloat16),
        "mp",
        scatter_dimension=0,
        tiled=True,
    ).astype(jnp.float32)
    pre_second = down_share + down_bias.astype(jnp.float32) + normed
    result, second_pull = jax.vjp(
        norm_rows, pre_second, second_gain.astype(jnp.float32), second_shift.astype(jnp.float32)
    )
    d_pre_second, second_gain_grad, second_shift_grad = second_pull(cotangent.astype(jnp.float32))
    down_bias_grad = jnp.sum(d_pre_second, axis=0)
    d_down = d_pre_second.astype(jnp.bfloat16)
    part_rows = lax.all_gather(d_down, "mp", axis=0, tiled=True)
    row_count = part_rows.shape[0]
    weight_acc = left_product(take_rows(act_low, jnp.int32(0), row_count), part_rows)
    act_grad = right_product(part_rows, down_weight)
    down_weight_grad, act_grad = (weight_acc, act_grad)
    d_inner = gelu_pull(act_grad)[0].astype(jnp.bfloat16)
    up_bias_grad = jnp.sum(d_inner.astype(jnp.float32), axis=0)
    up_weight_grad = left_product(gathered, d_inner)
    d_normed = (
        lax.psum_scatter(
            right_product(
                take_rows(d_inner, jnp.int32(0), share_rows * lax.axis_size("mp")), up_weight
            ).astype(jnp.bfloat16),
            "mp",
            scatter_dimension=0,
            tiled=True,
        ).astype(jnp.float32)
        + d_pre_second
    )
    d_pre_first, first_gain_grad, first_shift_grad = first_pull(d_normed)
    out_bias_grad = jnp.sum(d_pre_first, axis=0)
    d_attn = d_pre_first.astype(jnp.bfloat16)
    part_rows = lax.all_gather(d_attn, "mp", axis=0, tiled=True)
    row_count = part_rows.shape[0]
    weight_acc = left_product(take_rows(context, jnp.int32(0), row_count), part_rows)
    ctx_grad = right_product(part_rows, out_weight)
    out_weight_grad, ctx_grad = (weight_acc, ctx_grad)
    d_context = ctx_grad.astype(jnp.bfloat16)
    d_query, d_key, d_value, key_rows_grad, query_rows_grad = attn_bwd(
        queries, keys_all, values_all, key_rows, query_rows_up, probs, d_context
    )
    d_pos_query = jnp.dot(
        query_rows_grad.astype(jnp.bfloat16), hot_rising, preferred_element_type=jnp.float32
    ).T
    d_pos_key = jnp.dot(
        key_rows_grad.astype(jnp.bfloat16), hot_falling, preferred_element_type=jnp.float32
    ).T
    query_weight_grad = left_product(hidden_in, d_query) + left_wide(position_table, d_pos_query)
    key_weight_grad = left_product(hidden_in, d_key) + left_wide(position_table, d_pos_key)
    value_weight_grad = left_product(hidden_in, d_value)
    query_bias_grad = jnp.sum(d_query.astype(jnp.float32), axis=0) + jnp.sum(query_rows_grad, axis=1)
    key_bias_grad = jnp.sum(d_key.astype(jnp.float32), axis=0) + jnp.sum(key_rows_grad, axis=1)
    value_bias_grad = jnp.sum(d_value.astype(jnp.float32), axis=0)
    table_grad = right_wide(d_pos_query, query_weight) + right_wide(d_pos_key, key_weight)
    start_at = jnp.int32(0)
    input_grad = (
        lax.psum_scatter(
            (
                right_product(
                    take_rows(d_query, start_at, lax.axis_size("mp") * share_rows), query_weight
                )
                + right_product(
                    take_rows(d_key, start_at, lax.axis_size("mp") * share_rows), key_weight
                )
                + right_product(
                    take_rows(d_value, start_at, lax.axis_size("mp") * share_rows), value_weight
                )
            ).astype(jnp.bfloat16),
            "mp",
            scatter_dimension=0,
            tiled=True,
        ).astype(jnp.float32)
        + d_pre_first
    )
    (
        query_weight_grad,
        query_bias_grad,
        key_weight_grad,
        key_bias_grad,
        value_weight_grad,
        value_bias_grad,
        out_weight_grad,
        up_weight_grad,
        up_bias_grad,
        down_weight_grad,
    ) = (
        lax.psum(query_weight_grad.astype(jnp.bfloat16), "dp").astype(jnp.float32),
        lax.psum(query_bias_grad.astype(jnp.bfloat16), "dp").astype(jnp.float32),
        lax.psum(key_weight_grad.astype(jnp.bfloat16), "dp").astype(jnp.float32),
        lax.psum(key_bias_grad.astype(jnp.bfloat16), "dp").astype(jnp.float32),
        lax.psum(value_weight_grad.astype(jnp.bfloat16), "dp").astype(jnp.float32),
        lax.psum(value_bias_grad.astype(jnp.bfloat16), "dp").astype(jnp.float32),
        lax.psum(out_weight_grad.astype(jnp.bfloat16), "dp").astype(jnp.float32),
        lax.psum(up_weight_grad.astype(jnp.bfloat16), "dp").astype(jnp.float32),
        lax.psum(up_bias_grad.astype(jnp.bfloat16), "dp").astype(jnp.float32),
        lax.psum(down_weight_grad.astype(jnp.bfloat16), "dp").astype(jnp.float32),
    )
    (
        table_grad,
        out_bias_grad,
        first_gain_grad,
        first_shift_grad,
        down_bias_grad,
        second_gain_grad,
        second_shift_grad,
    ) = lax.psum(
        (
            table_grad,
            out_bias_grad,
            first_gain_grad,
            first_shift_grad,
            down_bias_grad,
            second_gain_grad,
            second_shift_grad,
        ),
        ("dp", "mp"),
    )
    return (
        result.astype(jnp.bfloat16),
        input_grad,
        table_grad,
        query_weight_grad,
        query_bias_grad,
        key_weight_grad,
        key_bias_grad,
        value_weight_grad,
        value_bias_grad,
        out_weight_grad,
        out_bias_grad,
        first_gain_grad,
        first_shift_grad,
        up_weight_grad,
        up_bias_grad,
        down_weight_grad,
        down_bias_grad,
        second_gain_grad,
        second_shift_grad,
    )


def solution(mesh):
    return jax.shard_map(
        on_device,
        mesh=mesh,
        in_specs=(
            P("dp", None),
            P("dp"),
            P(),
            P(),
            P(None, "mp"),
            P("mp"),
            P(None, "mp"),
            P("mp"),
            P(None, "mp"),
            P("mp"),
            P("mp", None),
            P(),
            P(),
            P(),
            P(None, "mp"),
            P("mp"),
            P("mp", None),
            P(),
            P(),
            P(),
            P(("dp", "mp"), None),
        ),
        out_specs=(
            P(("dp", "mp"), None),
            P(("dp", "mp"), None),
            P(),
            P(None, "mp"),
            P("mp"),
            P(None, "mp"),
            P("mp"),
            P(None, "mp"),
            P("mp"),
            P("mp", None),
            P(),
            P(),
            P(),
            P(None, "mp"),
            P("mp"),
            P("mp", None),
            P(),
            P(),
            P(),
        ),
        check_vma=False,
    )
```

time: 4200 us -> 753 us (0.18)
  other arithmetic: 2260 us -> 34.3 us
  local copies, waits for them, and re-layouts: 998 us -> 17.4 us
  matrix products: 271 us -> 82.5 us
  waiting for transfers between devices: 562 us -> 460 us
  Pallas kernels: 0 us -> 83 us
    select_n x106 -> x0, other arithmetic: 1550 us -> none  [shear_rows(): current = jnp.where(chosen, moved, current)]
    slice x103 -> x1, local copies, waits for them, and re-layouts: 811 us -> 1.34 us  [on_device(): falling = jnp.concatenate([bucket_of_offset[:1], bucket_of_offset[::-1]])]
    add_any x34 -> x0, other arithmetic: 531 us -> none  [shear_rows(): moved = jnp.concatenate([current[..., step_size:], filler], axis=-1)]
    dot_general x32 -> x6, matrix products: 184 us -> 13.3 us  [the longest x3 7.31 us: expand(): jnp.dot(one_hot, rows, preferred_element_type=jnp.float32)]
    while x350 -> x0, local copies, waits for them, and re-layouts: 157 us -> none
    pallas_call x0 -> x2, Pallas kernels: none -> 83 us  [the longest x1 49.5 us: attn_bwd(): pl.pallas_call(bwd_kernel, grid=(pairs,), in_specs=[col, col, col, rows,...]
    convert_element_type x7 -> x1, other arithmetic: 62.3 us -> 0.92 us  [on_device(): d_down = d_pre_second.astype(jnp.bfloat16)]
  transfers between devices with their start and end apart: 9 -> 9, of which waited for: 9 -> 9; matrix products, arithmetic and copies ran while one was open for 1% -> 6% of each run, Pallas kernels for 0% -> 0%
where the time goes in v1:
time: 753 us; the launch traced here: 747 us
  waiting for transfers between devices  460 us (61%)
  Pallas kernels  83 us (11%)
  matrix products  82.5 us (11%)
  blocking collectives  54 us (7%)
  other arithmetic  34.3 us (5%)
  local copies, waits for them, and re-layouts  17.4 us (2%)
  between operations  14.9 us (2%)
    psum x1, waiting for transfers between devices, on_device(): lax.psum((table_grad, out_bias_grad, first_gain_grad, first_shift_grad, d...  137 us
    pallas_call x1, Pallas kernels, attn_bwd(): pl.pallas_call(bwd_kernel, grid=(pairs,), in_specs=[col, col, col, rows,...  49.5 us
    reduce_scatter x1, waiting for transfers between devices, on_device(): lax.psum_scatter(jnp.dot(take_rows(context, jnp.int32(0), share_rows * la...  46.6 us
    all_gather x1, waiting for transfers between devices, on_device(): part_rows = lax.all_gather(d_down, 'mp', axis=0, tiled=True)  45.2 us
    all_gather x1, waiting for transfers between devices, on_device(): gathered = lax.all_gather(normed_low, 'mp', axis=0, tiled=True)  45.2 us
    reduce_scatter x1, waiting for transfers between devices, on_device(): lax.psum_scatter(right_product(take_rows(d_inner, jnp.int32(0), share_row...  42.7 us
    reduce_scatter x1, waiting for transfers between devices, on_device(): lax.psum_scatter(jnp.dot(take_rows(act_low, jnp.int32(0), share_rows * la...  42.6 us
    psum x1, blocking collectives, on_device(): lax.psum((table_grad, out_bias_grad, first_gain_grad, first_shift_grad, d...  40.6 us
  transfers between devices with their start and end apart: 9, of which 9 were waited for; matrix products, arithmetic and copies ran while one was open for 6% of the time, Pallas kernels for 0%

profile of v1, /device:TPU:0, one launch (start us, length us, event | category | flops | bytes accessed | tf_op | source)
XLA Modules:
  0.0 746.7 jit_solution(6496729333031748811)
XLA Ops:
  7.3 1.3 slice.4
  10.8 1.9 fusion.36
  12.7 3.2 fusion.27.q_ref
  16.7 1.5 fusion.28.k_ref
  18.2 3.6 fusion.11.kr_ref
  21.8 1.8 fusion.12.qr_ref
  23.7 1.5 fusion.29.v_ref
  25.2 33.5 %shard_map.348 = (bf16[4,1024,1024]{2,1,0:T(8,128)(2,1)}, bf16[1024,256]{1,0:T(8,128)(2,1)}) custom-call(bf16[1024,256]{1,0:T(8,128)(2,1)} %fusion.27.q_ref, bf16[1024,256]{1,0:T(8,128)(2,1)} %fusion.28.k_ref, bf16[1024,256]{1,0:T(8,128)(2,1)} %fusion.29.v_ref, bf16[2048,256]{1,0:T(8,128)(2,1)} %fusion.11.kr_ref, bf16[2048,256]{1,0:T(8,128)(2,1)} %fusion.12.qr_ref, ...), custom_call_target="tpu_custom_call" | custom-call | tf_op jit(solution)/shard_map/pallas_call | solution.py:129
  58.8 3.1 convolution_convert_fusion.4
  62.0 46.6 %reduce-scatter.5.cloned.1.call-done = bf16[256,1024]{1,0:T(8,128)(2,1)} async-done(((bf16[1024,1024]{1,0:T(8,128)(2,1)}), bf16[256,1024]{1,0:T(8,128)(2,1)}) %reduce-scatter.5.cloned.1.call-update) | async-done | bytes 524304 | tf_op jit(solution)/shard_map/reduce_scatter | solution.py:278
  108.6 1.4 fusion.42
  110.0 1.5 multiply_reduce_fusion.3
  111.6 2.3 fusion.43
  114.2 45.2 %all-gather.4.cloned.1.call-done = bf16[1024,1024]{1,0:T(8,128)(2,1)} async-done(((bf16[256,1024]{1,0:T(8,128)(2,1)}), bf16[1024,1024]{1,0:T(8,128)(2,1)}) %all-gather.4.cloned.1.call-update) | async-done | bytes 2097168 | tf_op jit(solution)/shard_map/all_gather | solution.py:294
  159.3 14.1 %multiply_convert_fusion = (bf16[1024,1024]{1,0:T(8,128)(2,1)S(1)}, f32[1024,1024]{1,0:T(8,128)}, f32[1024,1024]{1,0:T(8,128)}) fusion(f32[1024]{0:T(1024)S(1)} %convert_element_type.229, bf16[1024,1024]{1,0:T(8,128)(2,1)} %all-gather.4.cloned.1.call-done, bf16[1024,1024]{1,0:T(8,128)(2,1)S(1)} %copy-done), kind=kOutput, calls=%fused_computation.7 | convolution fusion | flops 2216689664 | bytes 14684160 | tf_op jit(solution)/shard_map/dot_general | solution.py:295
  173.4 1.4 copy-done.45
  174.8 3.7 convolution_convert_fusion.3
  178.6 42.6 %reduce-scatter.7.cloned.1.call-done = bf16[256,1024]{1,0:T(8,128)(2,1)} async-done(((bf16[1024,1024]{1,0:T(8,128)(2,1)}), bf16[256,1024]{1,0:T(8,128)(2,1)}) %reduce-scatter.7.cloned.1.call-update) | async-done | bytes 524304 | tf_op jit(solution)/shard_map/reduce_scatter | solution.py:300
  221.2 1.7 fusion.60
  223.7 1.3 fusion.59
  225.0 1.0 copy-done.6
  225.9 0.9 add_convert_fusion.4
  227.1 45.2 %all-gather.6.cloned.1.call-done = bf16[1024,1024]{1,0:T(8,128)(2,1)} async-done(((bf16[256,1024]{1,0:T(8,128)(2,1)}), bf16[1024,1024]{1,0:T(8,128)(2,1)}) %all-gather.6.cloned.1.call-update) | async-done | bytes 2097168 | tf_op jit(solution)/shard_map/all_gather | solution.py:317
  272.3 8.3 %fusion.57 = (bf16[1024]{0:T(1024)(128)(2,1)S(1)}, bf16[1024,1024]{1,0:T(8,128)(2,1)S(1)}) fusion(f32[1024,1024]{1,0:T(8,128)} %get-tuple-element.84, f32[1024,1024]{1,0:T(8,128)} %get-tuple-element.88, f32[1024]{0:T(1024)S(1)} %convert_element_type.229, bf16[1024,1024]{1,0:T(8,128)(2,1)} %all-gather.6.cloned.1.call-done, bf16[1024,1024]{1,0:T(8,128)(2,1)} %param.37), kind=kOutput, calls=%fused_computation.120 | convolution fusion | flops 2164259840 | bytes 14686208 | tf_op jit(solution)/shard_map/dot_general | solution.py:45
  280.6 1.3 copy-done.47
  282.0 3.7 convolution_convert_fusion.2
  285.7 42.7 %reduce-scatter.9.cloned.1.call-done = bf16[256,1024]{1,0:T(8,128)(2,1)} async-done(((bf16[1024,1024]{1,0:T(8,128)(2,1)}), bf16[256,1024]{1,0:T(8,128)(2,1)}) %reduce-scatter.9.cloned.1.call-update) | async-done | bytes 524304 | tf_op jit(solution)/shard_map/reduce_scatter | solution.py:326
  328.4 2.2 multiply_reduce_fusion
  330.6 2.0 fusion.58
  332.7 1.0 copy-done.9
  333.6 0.9 add_reduce_fusion
  335.8 1.8 fusion.13.qr_ref
  337.7 3.8 convolution_convert_fusion
  341.5 3.8 convolution_convert_fusion.1
  345.2 34.8 %all-gather.8.cloned.1.call-done = bf16[1024,1024]{1,0:T(8,128)(2,1)} async-done(((bf16[256,1024]{1,0:T(8,128)(2,1)}), bf16[1024,1024]{1,0:T(8,128)(2,1)}) %all-gather.8.cloned.1.call-update) | async-done | bytes 2097168 | tf_op jit(solution)/shard_map/all_gather | solution.py:339
  380.0 3.1 convolution_convert_fusion.7.dc_ref
  383.2 49.5 %shard_map.349 = (bf16[1024,256]{1,0:T(8,128)(2,1)}, bf16[1024,256]{1,0:T(8,128)(2,1)}, bf16[1024,256]{1,0:T(8,128)(2,1)}, f32[256,2048]{1,0:T(8,128)}, f32[256,2048]{1,0:T(8,128)}) custom-call(bf16[1024,256]{1,0:T(8,128)(2,1)} %fusion.27.q_ref, bf16[1024,256]{1,0:T(8,128)(2,1)} %fusion.28.k_ref, bf16[1024,256]{1,0:T(8,128)(2,1)} %fusion.29.v_ref, ...), custom_call_target="tpu_custom_call" | custom-call | tf_op jit(solution)/shard_map/pallas_call | solution.py:207
  432.7 2.8 fusion.14
  437.1 1.2 fusion.16
  439.5 1.5 fusion.32
  441.0 1.3 fusion.33
  442.3 1.3 fusion.34
  443.6 1.5 convolution_convert_fusion.5
  445.3 1.9 fusion.62
  448.0 2.1 add_convert_fusion
  450.2 1.7 fusion.49
  452.0 1.5 fusion.53
  453.5 1.5 fusion.55
  455.0 1.9 add_add_fusion
  457.0 40.6 %all-reduce = (f32[1024]{0:T(1024)}, f32[1024]{0:T(1024)}, f32[1024]{0:T(1024)}, f32[1024]{0:T(1024)}, f32[1024]{0:T(1024)}, /*index=5*/f32[1024]{0:T(1024)}) all-reduce(f32[1024]{0:T(1024)S(1)} %get-tuple-element.86, f32[1024]{0:T(1024)S(1)} %get-tuple-element.52, ...), channel_id=1, replica_groups=mesh['dp'=8,'mp'=4] {'dp','mp'}, use_global_device_ids=true, to_apply=%region_26.0 | all-reduce | flops 6144 | bytes 49152 | tf_op jit(solution)/shard_map/psum | solution.py:412
  497.6 1.8 reduce_sum.229
  499.3 1.8 reduce_sum.227
  501.5 13.4 %all-reduce.1 = (bf16[256]{0:T(256)(128)(2,1)S(1)}, bf16[256]{0:T(256)(128)(2,1)S(1)}, bf16[256]{0:T(256)(128)(2,1)S(1)}, bf16[1024]{0:T(1024)(128)(2,1)S(1)}) all-reduce(bf16[256]{0:T(256)(128)(2,1)S(1)} %add_convert_fusion.6, bf16[256]{0:T(256)(128)(2,1)S(1)} %add_convert_fusion.5, ...), channel_id=1, replica_groups=mesh['dp'=8,'mp'=4] {'dp'}, use_global_device_ids=true, to_apply=%region_16.0 | all-reduce | flops 1792 | bytes 7168 | tf_op jit(solution)/shard_map/psum | solution.py:394
  517.2 33.6 %all-reduce.8.cloned.1.call-done = (bf16[1024,256]{0,1:T(8,128)(2,1)}, bf16[1024,256]{0,1:T(8,128)(2,1)}, bf16[1024,256]{0,1:T(8,128)(2,1)}, bf16[256,1024]{1,0:...) async-done(((bf16[1024,256]{0,1:T(8,128)(2,1)}, bf16[1024,256]{0,1:T(8,128)(2,1)}, bf16[1024,256]{0,1:T(8,128)(2,1)}, bf16[256,1024]{1,0:T(8,128)(2,1)}, ...) | async-done | bytes 6291472 | tf_op jit(solution)/shard_map/psum | solution.py:393
  550.8 4.2 convert_element_type.274
  555.0 2.5 convert_element_type.277
  557.5 1.1 convert_element_type.272
  558.6 2.3 copy.40
  560.9 2.2 copy.41
  563.2 2.4 copy.42
  565.5 31.6 %reduce-scatter.11.cloned.1.call-done = bf16[256,1024]{1,0:T(8,128)(2,1)} async-done(((bf16[1024,1024]{1,0:T(8,128)(2,1)}), bf16[256,1024]{1,0:T(8,128)(2,1)}) %reduce-scatter.11.cloned.1.call-update) | async-done | bytes 524304 | tf_op jit(solution)/shard_map/reduce_scatter | solution.py:363
  597.1 2.2 convert_add_fusion
  599.3 137.2 %all-reduce.6.cloned.1.call-done = f32[512,1024]{1,0:T(8,128)} async-done(((f32[512,1024]{1,0:T(8,128)}), f32[512,1024]{1,0:T(8,128)}) %all-reduce.6.cloned.1.call-update) | async-done | bytes 2097168 | tf_op jit(solution)/shard_map/psum | solution.py:412
  736.5 3.2 copy.50
  (149 shorter events, 12.1 us)
Async XLA Ops:
  7.2 152.1 %copy-start = (bf16[1024,1024]{1,0:T(8,128)(2,1)S(1)}, bf16[1024,1024]{1,0:T(8,128)(2,1)}, u32[]{:S(2)}) copy-start(bf16[1024,1024]{1,0:T(8,128)(2,1)} %param.35) | copy-start | bytes 6291460
  7.2 101.4 %reduce-scatter.5.cloned.1.call-start = ((), (), s32[]{:S(2)}) async-start(), calls=%async_computation.4 | async-start | bytes 2621440 | tf_op jit(solution)/shard_map/reduce_scatter | solution.py:278
  10.8 5.9 copy-start.2
  10.8 5.9 copy-start.17
  15.9 2.3 copy-start.7
  18.2 5.5 copy-start.44
  21.8 1.9 copy-start.3
  21.8 1.9 copy-start.28
  23.7 35.0 %copy-start.31 = (bf16[256,1024]{1,0:T(8,128)(2,1)S(1)}, bf16[256,1024]{1,0:T(8,128)(2,1)}, u32[]{:S(2)}) copy-start(bf16[256,1024]{1,0:T(8,128)(2,1)} %param.31) | copy-start | bytes 1572868
  25.2 36.7 %copy-start.34 = (bf16[1024]{0:T(1024)(128)(2,1)S(1)}, bf16[1024]{0:T(1024)(128)(2,1)}, u32[]{:S(2)}) copy-start(bf16[1024]{0:T(1024)(128)(2,1)} %param.32) | copy-start | bytes 6148
  25.2 36.7 %copy-start.35 = (bf16[1024]{0:T(1024)(128)(2,1)S(1)}, bf16[1024]{0:T(1024)(128)(2,1)}, u32[]{:S(2)}) copy-start(bf16[1024]{0:T(1024)(128)(2,1)} %param.33) | copy-start | bytes 6148
  25.2 36.7 %copy-start.36 = (bf16[1024]{0:T(1024)(128)(2,1)S(1)}, bf16[1024]{0:T(1024)(128)(2,1)}, u32[]{:S(2)}) copy-start(bf16[1024]{0:T(1024)(128)(2,1)} %param.34) | copy-start | bytes 6148
  58.7 55.4 %copy-start.37 = (bf16[1024]{0:T(1024)(128)(2,1)S(1)}, bf16[1024]{0:T(1024)(128)(2,1)}, u32[]{:S(2)}) copy-start(bf16[1024]{0:T(1024)(128)(2,1)} %param.36) | copy-start | bytes 6148
  61.9 97.5 %all-gather.4.cloned.1.call-start = ((), (), s32[]{:S(2)}) async-start(), calls=%async_computation.5 | async-start | bytes 2621440 | tf_op jit(solution)/shard_map/all_gather | solution.py:294
  113.9 107.3 %reduce-scatter.7.cloned.1.call-start = ((), (), s32[]{:S(2)}) async-start(), calls=%async_computation.6 | async-start | bytes 2621440 | tf_op jit(solution)/shard_map/reduce_scatter | solution.py:300
  159.3 15.5 %copy-start.41 = (bf16[1024,1024]{1,0:T(8,128)(2,1)S(1)}, bf16[1024,1024]{1,0:T(8,128)(2,1)}, u32[]{:S(2)}) copy-start(bf16[1024,1024]{1,0:T(8,128)(2,1)} %param.37) | copy-start | bytes 6291460
  173.4 1.4 copy-start.45
  174.8 3.8 copy-start.38
  174.8 3.8 copy-start.39
  174.8 3.8 copy-start.40
  174.8 46.4 %copy-start.5 = (bf16[256,1024]{1,0:T(8,128)(2,1)S(1)}, bf16[256,1024]{1,0:T(8,128)(2,1)}, u32[]{:S(2)}) copy-start(bf16[256,1024]{1,0:T(8,128)(2,1)} %reduce-scatter.5.cloned.1.call-done) | copy-start | bytes 1572868
  178.5 44.8 %copy-start.26 = (bf16[256,1024]{1,0:T(8,128)(2,1)S(1)}, bf16[256,1024]{1,0:T(8,128)(2,1)}, u32[]{:S(2)}) copy-start(bf16[256,1024]{1,0:T(8,128)(2,1)} %param.41) | copy-start | bytes 1572868
  178.5 93.8 %all-gather.6.cloned.1.call-start = ((), (), s32[]{:S(2)}) async-start(), calls=%async_computation.7 | async-start | bytes 2621440 | tf_op jit(solution)/shard_map/all_gather | solution.py:317
  224.9 1.0 copy-start.6
  226.9 101.5 %reduce-scatter.9.cloned.1.call-start = ((), (), s32[]{:S(2)}) async-start(), calls=%async_computation.8 | async-start | bytes 2621440 | tf_op jit(solution)/shard_map/reduce_scatter | solution.py:326
  280.6 1.3 copy-start.47
  285.7 45.0 %copy-start.4 = (bf16[1024,1024]{1,0:T(8,128)(2,1)S(1)}, bf16[1024,1024]{1,0:T(8,128)(2,1)}, u32[]{:S(2)}) copy-start(bf16[1024,1024]{1,0:T(8,128)(2,1)} %param.21) | copy-start | bytes 6291460
  285.7 49.2 %copy-start.33 = (s32[2047]{0:T(1024)S(1)}, s32[2047]{0:T(1024)}, u32[]{:S(2)}) copy-start(s32[2047]{0:T(1024)} %param.23) | copy-start | bytes 24568
  285.7 94.3 %all-gather.8.cloned.1.call-start = ((), (), s32[]{:S(2)}) async-start(), calls=%async_computation.9 | async-start | bytes 2621440 | tf_op jit(solution)/shard_map/all_gather | solution.py:339
  332.6 1.0 copy-start.9
  334.6 216.2 %all-reduce.8.cloned.1.call-start = ((), (), s32[]{:S(2)}) async-start(), calls=%async_computation.12 | async-start | bytes 12582912 | tf_op jit(solution)/shard_map/psum | solution.py:393
  334.9 2.7 copy-start.43
  334.9 2.7 copy-start.46
  337.6 3.8 copy-start.42
  337.6 3.8 copy-start.48
  341.5 38.6 %copy-start.32 = (bf16[256,1024]{1,0:T(8,128)(2,1)S(1)}, bf16[256,1024]{1,0:T(8,128)(2,1)}, u32[]{:S(2)}) copy-start(bf16[256,1024]{1,0:T(8,128)(2,1)} %param.31) | copy-start | bytes 1572868
  432.6 2.9 copy-start.8
  432.6 3.4 copy-start.14
  435.5 1.6 copy-start.25
  436.7 2.0 copy-start.11
  438.3 1.2 copy-start.20
  441.0 2.6 copy-start.24
  441.0 2.6 copy-start.27
  443.6 1.6 copy-start.12
  445.2 2.0 copy-start.15
  445.2 2.0 copy-start.18
  445.2 2.8 copy-start.21
  445.2 151.9 %reduce-scatter.11.cloned.1.call-start = ((), (), s32[]{:S(2)}) async-start(), calls=%async_computation.10 | async-start | bytes 2621440 | tf_op jit(solution)/shard_map/reduce_scatter | solution.py:363
  445.3 2.7 copy-start.29
  450.2 286.3 %all-reduce.6.cloned.1.call-start = ((), (), s32[]{:S(2)}) async-start(), calls=%async_computation.11 | async-start | bytes 4194304 | tf_op jit(solution)/shard_map/psum | solution.py:412
  450.2 4.8 copy-start.19
  456.9 44.2 %copy-start.22 = (bf16[1024,256]{1,0:T(8,128)(2,1)S(1)}, bf16[1024,256]{1,0:T(8,128)(2,1)}, u32[]{:S(2)}) copy-start(bf16[1024,256]{1,0:T(8,128)(2,1)} %get-tuple-element.30) | copy-start | bytes 1572868
  456.9 44.3 %copy-start.13 = (bf16[1024,256]{1,0:T(8,128)(2,1)S(1)}, bf16[1024,256]{1,0:T(8,128)(2,1)}, u32[]{:S(2)}) copy-start(bf16[1024,256]{1,0:T(8,128)(2,1)} %get-tuple-element.28) | copy-start | bytes 1572868
  456.9 44.3 %copy-start.16 = (bf16[1024,256]{1,0:T(8,128)(2,1)S(1)}, bf16[1024,256]{1,0:T(8,128)(2,1)}, u32[]{:S(2)}) copy-start(bf16[1024,256]{1,0:T(8,128)(2,1)} %get-tuple-element.29) | copy-start | bytes 1572868
  550.8 4.2 copy-start.23
  555.0 2.5 copy-start.30
  557.5 39.6 %copy-start.10 = (f32[256,1024]{1,0:T(8,128)S(1)}, f32[256,1024]{1,0:T(8,128)}, u32[]{:S(2)}) copy-start(f32[256,1024]{1,0:T(8,128)} %copy-done.9) | copy-start | bytes 3145732
  563.1 176.5 %copy-start.1 = (bf16[1024,1024]{1,0:T(8,128)(2,1)S(1)}, bf16[1024,1024]{1,0:T(8,128)(2,1)}, u32[]{:S(2)}) copy-start(bf16[1024,1024]{1,0:T(8,128)(2,1)} %param.35) | copy-start | bytes 6291460
Sparse Core Ops, SparseCore 0:
  62.0 46.5 reduce-scatter.4
  114.0 45.2 all-gather.3
  178.6 42.5 reduce-scatter.6
  227.0 45.2 all-gather.5
  285.8 42.5 reduce-scatter.8
  334.7 45.2 all-gather.7
  445.3 105.4 all-reduce.7
  553.1 43.9 reduce-scatter.10
  603.3 133.1 all-reduce.5

commit v2 on v0

v2 whole, which is shorter than its diff:
```python
import functools
import math

import jax
import jax.numpy as jnp
from jax import lax
from jax.experimental import pallas as pl
from jax.experimental.pallas import tpu as pltpu
from jax.sharding import PartitionSpec as P

HEAD = 64
PAIR = 2 * HEAD
LEN = 1024
BLK = 128

NORM_EPS = 1e-07
MASK_FILL = -1000000000.0
SCALE = 1.0 / math.sqrt(3.0 * HEAD)

F32 = jnp.float32
BF16 = jnp.bfloat16

NN = (((1,), (0,)), ((), ()))
NT = (((1,), (1,)), ((), ()))
TN = (((0,), (0,)), ((), ()))


def dot(left, right, dims=NN):
    return lax.dot_general(left, right, dims, preferred_element_type=F32)


def ordered(kernel, inputs, deps):
    def body(*refs):
        kernel(*refs[:inputs], *refs[inputs + len(deps) :])

    return body


def half_of(values, half):
    lane = lax.broadcasted_iota(jnp.int32, (1, PAIR), 1)
    return jnp.where((lane >= HEAD) if half else (lane < HEAD), values, jnp.zeros_like(values))


def join_halves(first, second):
    lane = lax.broadcasted_iota(jnp.int32, (1, PAIR), 1)
    return jnp.where(lane < HEAD, first, second)


def unit_matrix(flipped):
    row = lax.broadcasted_iota(jnp.int32, (BLK, BLK), 0)
    col = lax.broadcasted_iota(jnp.int32, (BLK, BLK), 1)
    hit = (row + col == BLK - 1) if flipped else (row == col)
    return hit.astype(F32).astype(BF16)


def shear(values):
    return pltpu.roll(values, 0, 1, stride=1, stride_axis=0)[:, BLK:]


def spread(values, base):
    wide = jnp.concatenate([values, jnp.zeros((values.shape[0], BLK), values.dtype)], axis=1)
    return pltpu.roll(wide, base, 1, stride=1, stride_axis=0)


def fwd_kernel(q_ref, k_ref, v_ref, kr_ref, qr_ref, mask_ref, p_ref, ctx_ref, from_scr):
    length = k_ref.shape[0]
    span = length + BLK
    step = pl.program_id(0)

    @pl.when(step == 0)
    def _():
        def from_rows(b, carry):
            j0 = pl.multiple_of(b * BLK, BLK)
            slab = qr_ref[pl.ds(pl.multiple_of(length - BLK - j0, BLK), span), :]
            kb = k_ref[pl.ds(j0, BLK), :]
            for half in (0, 1):
                part = dot(half_of(kb, half), slab, NT)
                from_scr[half, pl.ds(j0, BLK), :] = shear(part).astype(BF16)
            return carry

        lax.fori_loop(0, length // BLK, from_rows, 0)

    ident = unit_matrix(False)
    live = mask_ref[...] > 0
    i0 = pl.multiple_of(step * BLK, BLK)
    slab = kr_ref[pl.ds(pl.multiple_of(length - BLK - i0, BLK), span), :]
    qb = q_ref[pl.ds(i0, BLK), :]
    parts = []
    for half in (0, 1):
        qm = half_of(qb, half)
        to_pos = shear(dot(qm, slab, NT))
        left = jnp.concatenate([ident, qm], axis=1)
        right = jnp.concatenate([from_scr[half, :, pl.ds(i0, BLK)], k_ref[...]], axis=1)
        score = (dot(left, right, NT) + to_pos) * SCALE
        score = jnp.where(live, score, MASK_FILL)
        expd = jnp.exp(score - jnp.max(score, axis=1, keepdims=True))
        prob = (expd * (1.0 / jnp.sum(expd, axis=1, keepdims=True))).astype(BF16)
        p_ref[half] = prob
        parts.append(dot(prob, v_ref[...]))
    ctx_ref[...] = join_halves(parts[0], parts[1]).astype(BF16)


def attn_fwd(pair, q, k, v, kr, qr, mask, deps=()):
    length = q.shape[0]
    col = pl.BlockSpec((length, PAIR), lambda i: (0, pair))
    rows = pl.BlockSpec((2 * length, PAIR), lambda i: (0, pair))
    return pl.pallas_call(
        ordered(fwd_kernel, 6, deps),
        grid=(length // BLK,),
        in_specs=[col, col, col, rows, rows, pl.BlockSpec((1, length), lambda i: (0, 0))]
        + [pl.BlockSpec(memory_space=pl.ANY)] * len(deps),
        out_specs=[
            pl.BlockSpec((2, BLK, length), lambda i: (0, i, 0)),
            pl.BlockSpec((BLK, PAIR), lambda i: (i, 0)),
        ],
        out_shape=[
            pltpu.HBM((2, length, length), BF16),
            jax.ShapeDtypeStruct((length, PAIR), BF16),
        ],
        scratch_shapes=[pltpu.VMEM((2, length, length), BF16)],
        compiler_params=pltpu.CompilerParams(vmem_limit_bytes=40 * 2**20),
        cost_estimate=pl.CostEstimate(
            flops=128 * length * length * PAIR, bytes_accessed=10 * 2**20, transcendentals=2 * length * length
        ),
        name="attn_fwd",
    )(q, k, v, kr, qr, mask, *deps)


def bwd_rows_kernel(
    q_ref, k_ref, v_ref, kr_ref, p_ref, dc_ref, dq_ref, dv_ref, dkr_ref, ds_ref, qrev_ref, dv_scr, dkr_scr
):
    length = k_ref.shape[0]
    span = length + BLK
    step = pl.program_id(0)
    last = pl.num_programs(0) - 1

    @pl.when(step == 0)
    def _():
        dv_scr[...] = jnp.zeros_like(dv_scr)
        dkr_scr[...] = jnp.zeros_like(dkr_scr)

    rev = unit_matrix(True)
    i0 = pl.multiple_of(step * BLK, BLK)
    u0 = pl.multiple_of(length - BLK - i0, BLK)
    slab = kr_ref[pl.ds(u0, span), :]
    qb = dot(rev, q_ref[pl.ds(i0, BLK), :]).astype(BF16)
    qrev_ref[...] = qb
    dcb = dc_ref[pl.ds(i0, BLK), :]
    dcr = dot(rev, dcb).astype(BF16)
    parts = []
    dv_part = 0.0
    dkr_part = 0.0
    for half in (0, 1):
        prob = p_ref[half]
        d_prob = dot(half_of(dcr, half), v_ref[...], NT)
        prob_rev = dot(rev, prob)
        weighted = prob_rev * d_prob
        d_score = weighted - prob_rev * jnp.sum(weighted, axis=1, keepdims=True)
        d_low = d_score.astype(BF16)
        ds_ref[half] = d_low
        d_to = spread(d_score, 1).astype(BF16)
        parts.append(dot(d_low, k_ref[...]) + dot(d_to, slab))
        dv_part = dv_part + dot(half_of(dcb, half), prob, TN)
        dkr_part = dkr_part + dot(half_of(qb, half), d_to, TN)
    dqb = (join_halves(parts[0], parts[1]) * SCALE).astype(BF16)
    dq_ref[...] = dot(rev, dqb).astype(BF16)
    dv_scr[...] += dv_part
    dkr_scr[:, pl.ds(u0, span)] += dkr_part

    @pl.when(step == last)
    def _():
        dv_ref[...] = dv_scr[...].T.astype(BF16)
        dkr_ref[...] = (dkr_scr[...] * SCALE).astype(BF16)


def attn_bwd_rows(pair, q, k, v, kr, p, dc, deps=()):
    length = q.shape[0]
    steps = length // BLK
    col = pl.BlockSpec((length, PAIR), lambda i: (0, pair))
    whole = pl.BlockSpec((length, PAIR), lambda i: (0, 0))
    turned = pl.BlockSpec((BLK, PAIR), lambda i: (steps - 1 - i, 0))
    cols = jax.ShapeDtypeStruct((length, PAIR), BF16)
    return pl.pallas_call(
        ordered(bwd_rows_kernel, 6, deps),
        grid=(steps,),
        in_specs=[
            col,
            col,
            col,
            pl.BlockSpec((2 * length, PAIR), lambda i: (0, pair)),
            pl.BlockSpec((2, BLK, length), lambda i: (0, i, 0)),
            col,
        ]
        + [pl.BlockSpec(memory_space=pl.ANY)] * len(deps),
        out_specs=[
            pl.BlockSpec((BLK, PAIR), lambda i: (i, 0)),
            whole,
            pl.BlockSpec((PAIR, 2 * length), lambda i: (0, 0)),
            pl.BlockSpec((2, BLK, length), lambda i: (0, steps - 1 - i, 0)),
            turned,
        ],
        out_shape=[
            cols,
            cols,
            jax.ShapeDtypeStruct((PAIR, 2 * length), BF16),
            pltpu.HBM((2, length, length), BF16),
            cols,
        ],
        scratch_shapes=[pltpu.VMEM((PAIR, length), F32), pltpu.VMEM((PAIR, 2 * length), F32)],
        compiler_params=pltpu.CompilerParams(vmem_limit_bytes=40 * 2**20),
        cost_estimate=pl.CostEstimate(
            flops=128 * length * length * PAIR, bytes_accessed=10 * 2**20, transcendentals=0
        ),
        name="attn_bwd_rows",
    )(q, k, v, kr, p, dc, *deps)


def bwd_cols_kernel(k_ref, qr_ref, ds_ref, qrev_ref, dk_ref, dqr_ref, dqr_scr):
    length = k_ref.shape[0]
    span = length + BLK
    step = pl.program_id(0)
    last = pl.num_programs(0) - 1

    @pl.when(step == 0)
    def _():
        dqr_scr[...] = jnp.zeros_like(dqr_scr)

    ident = unit_matrix(False)
    j0 = pl.multiple_of(step * BLK, BLK)
    slab = qr_ref[pl.ds(j0, span), :]
    kb = k_ref[pl.ds(j0, BLK), :]
    parts = []
    dqr_part = 0.0
    for half in (0, 1):
        turned = dot(ident, ds_ref[half], NT)
        d_from = spread(turned, 0).astype(BF16)
        parts.append(dot(turned.astype(BF16), qrev_ref[...]) + dot(d_from, slab))
        dqr_part = dqr_part + dot(half_of(kb, half), d_from, TN)
    dk_ref[...] = (join_halves(parts[0], parts[1]) * SCALE).astype(BF16)
    dqr_scr[:, pl.ds(j0, span)] += dqr_part

    @pl.when(step == last)
    def _():
        dqr_ref[...] = (dqr_scr[...] * SCALE).astype(BF16)


def attn_bwd_cols(pair, k, qr, ds, qrev, deps=()):
    length = k.shape[0]
    return pl.pallas_call(
        ordered(bwd_cols_kernel, 4, deps),
        grid=(length // BLK,),
        in_specs=[
            pl.BlockSpec((length, PAIR), lambda i: (0, pair)),
            pl.BlockSpec((2 * length, PAIR), lambda i: (0, pair)),
            pl.BlockSpec((2, length, BLK), lambda i: (0, 0, i)),
            pl.BlockSpec((length, PAIR), lambda i: (0, 0)),
        ]
        + [pl.BlockSpec(memory_space=pl.ANY)] * len(deps),
        out_specs=[
            pl.BlockSpec((BLK, PAIR), lambda i: (i, 0)),
            pl.BlockSpec((PAIR, 2 * length), lambda i: (0, 0)),
        ],
        out_shape=[
            jax.ShapeDtypeStruct((length, PAIR), BF16),
            jax.ShapeDtypeStruct((PAIR, 2 * length), BF16),
        ],
        scratch_shapes=[pltpu.VMEM((PAIR, 2 * length), F32)],
        compiler_params=pltpu.CompilerParams(vmem_limit_bytes=40 * 2**20),
        cost_estimate=pl.CostEstimate(
            flops=88 * length * length * PAIR, bytes_accessed=10 * 2**20, transcendentals=0
        ),
        name="attn_bwd_cols",
    )(k, qr, ds, qrev, *deps)


def to_16(rows):
    more = -rows.shape[0] % 16
    if more:
        rows = jnp.concatenate([rows, jnp.zeros((more, rows.shape[1]), rows.dtype)], axis=0)
    return rows


def up_16(count):
    return count + -count % 16


def pack_kernel(parts, at_ref, *refs):
    d_refs, g_refs = refs[:6], refs[6:10]
    hidden_ref, table_ref, rising_ref, falling_ref, vec_ref, out_ref = refs[10:]
    table_rows = table_ref.shape[0]
    length = rising_ref.shape[1]
    bucket = lax.broadcasted_iota(jnp.int32, (table_rows, length), 0)
    weights = []
    positions = []
    biases = []
    for which in range(3):
        d_both = jnp.concatenate([d_refs[2 * which][...], d_refs[2 * which + 1][...]], axis=1)
        grad = dot(d_both, hidden_ref[...], TN)
        bias = jnp.sum(d_both.astype(F32), axis=0, keepdims=True)
        if which < 2:
            index_ref = (rising_ref, falling_ref)[which]
            hot = (bucket == index_ref[...]).astype(F32).astype(BF16)
            rows = jnp.concatenate([g_refs[2 * which][...], g_refs[2 * which + 1][...]], axis=0)
            pos = dot(hot, rows, NT)
            bias = bias + jnp.sum(pos, axis=0, keepdims=True)
            grad = grad + dot(pos.astype(BF16), table_ref[...], TN)
            positions.append(pos)
        weights.append(grad)
        biases.append(bias)
    weights = jnp.concatenate(weights, axis=0)
    positions = jnp.concatenate(positions, axis=1)
    width = weights.shape[1]
    biases = jnp.concatenate(biases, axis=1)
    biases = jnp.concatenate([biases, jnp.zeros((1, width - biases.shape[1]), F32)], axis=1)
    mine = lax.broadcasted_iota(jnp.int32, (16, width), 0) == at_ref[0]
    vectors = vec_ref[...] + jnp.where(mine, biases, 0.0)
    step = weights.shape[0] // parts
    half = table_rows // parts // 2
    for b in range(parts):
        pos = positions[2 * b * half : 2 * (b + 1) * half]
        out_ref[b] = jnp.concatenate(
            [
                to_16(weights[b * step : (b + 1) * step]),
                to_16(jnp.concatenate([pos[:half], pos[half:]], axis=1)),
                vectors if b == 0 else jnp.zeros_like(vectors),
            ],
            axis=0,
        ).astype(BF16)


def pack(parts, at, d_parts, grads, hidden, table, rising, falling, vectors, deps=()):
    width = hidden.shape[1]
    cols = 6 * PAIR
    rows = up_16(cols // parts) + up_16(table.shape[0] // parts // 2) + 16
    return pl.pallas_call(
        ordered(functools.partial(pack_kernel, parts), 16, deps),
        in_specs=[pl.BlockSpec(memory_space=pltpu.SMEM)]
        + [pl.BlockSpec(memory_space=pltpu.VMEM)] * 15
        + [pl.BlockSpec(memory_space=pl.ANY)] * len(deps),
        out_specs=pl.BlockSpec(memory_space=pltpu.VMEM),
        out_shape=jax.ShapeDtypeStruct((parts, rows, width), BF16),
        compiler_params=pltpu.CompilerParams(vmem_limit_bytes=48 * 2**20),
        cost_estimate=pl.CostEstimate(flops=8 * 10**9, bytes_accessed=10 * 2**20, transcendentals=0),
        name="pack",
    )(at, *d_parts, *grads, hidden, table, rising, falling, vectors, *deps)


def unpack_kernel(step, table_step, in_ref, q_ref, k_ref, v_ref, table_ref, vec_ref):
    parts = in_ref.shape[0]
    rows = up_16(step)
    weights = jnp.concatenate([in_ref[b, :rows].astype(F32)[:step] for b in range(parts)], axis=0)
    width = q_ref.shape[1]
    for i, ref in enumerate((q_ref, k_ref, v_ref)):
        ref[...] = weights[i * width : (i + 1) * width].T
    table = [in_ref[b, rows : rows + up_16(table_step)].astype(F32)[:table_step] for b in range(parts)]
    table_ref[...] = jnp.concatenate(table, axis=0)
    vec_ref[...] = in_ref[0, rows + up_16(table_step) :].astype(F32)


def unpack(whole, cols, table_rows):
    parts, _, width = whole.shape
    weight = jax.ShapeDtypeStruct((width, cols), F32)
    return pl.pallas_call(
        functools.partial(unpack_kernel, 3 * cols // parts, table_rows // parts),
        in_specs=[pl.BlockSpec(memory_space=pltpu.VMEM)],
        out_specs=[pl.BlockSpec(memory_space=pltpu.VMEM)] * 5,
        out_shape=[weight] * 3
        + [jax.ShapeDtypeStruct((table_rows, width), F32), jax.ShapeDtypeStruct((16, width), F32)],
        compiler_params=pltpu.CompilerParams(vmem_limit_bytes=48 * 2**20),
        name="unpack",
    )(whole)


def widen_kernel(in_ref, *refs):
    rows = in_ref[0].astype(F32)
    start = 0
    for ref in refs:
        ref[...] = rows[start : start + ref.shape[0]]
        start += ref.shape[0]


def widen(gathered, counts):
    parts, rows, width = gathered.shape
    return pl.pallas_call(
        widen_kernel,
        grid=(parts,),
        in_specs=[pl.BlockSpec((1, rows, width), lambda b: (b, 0, 0))],
        out_specs=[pl.BlockSpec((count, width), lambda b: (b, 0)) for count in counts],
        out_shape=[jax.ShapeDtypeStruct((parts * count, width), F32) for count in counts],
        cost_estimate=pl.CostEstimate(flops=0, bytes_accessed=6 * parts * rows * width, transcendentals=0),
        name="widen",
    )(gathered)


def swap(values, axis, mask):
    return lax.ppermute(values, axis, [(i, i ^ mask) for i in range(lax.axis_size(axis))])


def after(value, *deps):
    return lax.optimization_barrier((value, *deps))[0]


def pick(values, index, axis=0):
    return lax.dynamic_index_in_dim(values, index, axis, keepdims=False)


def bit_of(axis, mask):
    return (lax.axis_index(axis) & mask) // mask


def add_low(left, right):
    return (left.astype(F32) + right.astype(F32)).astype(BF16)


def pick_bit(values, at, low, bit):
    shape = values.shape
    cut = values.reshape(shape[:at] + (shape[at] // (2 * low), 2, low) + shape[at + 1 :])
    part = pick(cut, bit, at + 1)
    return part.reshape(shape[:at] + (shape[at] // 2,) + shape[at + 1 :])


def send_together(arrays, axis, mask):
    last = arrays[0].shape[-1]
    got = swap(jnp.concatenate([a.reshape(-1, last) for a in arrays], axis=0), axis, mask)
    parts = []
    start = 0
    for a in arrays:
        rows = a.size // last
        parts.append(got[start : start + rows].reshape(a.shape))
        start += rows
    return parts


def halve(arrays, ats, low, mask):
    bit = bit_of("dp", mask)
    theirs = send_together([pick_bit(a, at, low, 1 - bit) for a, at in zip(arrays, ats)], "dp", mask)
    return [pick_bit(a, at, low, bit) for a, at in zip(arrays, ats)], theirs


def add_all(pair):
    return [add_low(mine, theirs) for mine, theirs in zip(*pair)]


def low_sum_over(values, axis):
    mask = 1
    while mask < lax.axis_size(axis):
        values = add_low(values, swap(values, axis, mask))
        mask *= 2
    return values


def norm_parts(values):
    row_mean = jnp.mean(values, axis=-1, keepdims=True)
    centered = values - row_mean
    row_var = jnp.mean(centered * centered, axis=-1, keepdims=True)
    inverse = lax.rsqrt(row_var + NORM_EPS)
    return centered * inverse, inverse


def norm_back(grad, unit_rows, inverse, gain):
    d_unit = grad * gain
    mean_d = jnp.mean(d_unit, axis=-1, keepdims=True)
    mean_du = jnp.mean(d_unit * unit_rows, axis=-1, keepdims=True)
    return inverse * (d_unit - mean_d - unit_rows * mean_du)


def gelu_parts(values):
    cumulative = 0.5 + 0.5 * lax.erf(values * math.sqrt(0.5))
    density = jnp.exp(-0.5 * values * values) * (1.0 / math.sqrt(2.0 * math.pi))
    return values * cumulative, cumulative + values * density


def on_device(
    hidden_in,
    key_mask,
    bucket_of_offset,
    position_table,
    query_weight,
    query_bias,
    key_weight,
    key_bias,
    value_weight,
    value_bias,
    out_weight,
    out_bias,
    first_gain,
    first_shift,
    up_weight,
    up_bias,
    down_weight,
    down_bias,
    second_gain,
    second_shift,
    cotangent,
):
    tokens, width = hidden_in.shape
    width_loc = query_weight.shape[1]
    units = up_weight.shape[1]
    pairs = width_loc // PAIR
    dp_parts = lax.axis_size("dp")
    mp_parts = lax.axis_size("mp")
    dp_index = lax.axis_index("dp")
    mp_index = lax.axis_index("mp")
    share = tokens // mp_parts
    assert tokens == LEN and mp_parts == 4 and dp_parts & (dp_parts - 1) == 0
    dp_masks = [1 << b for b in range(dp_parts.bit_length() - 1)]
    others = range(1, mp_parts)

    def relative(blocks):
        return jnp.concatenate([pick(blocks, mp_index ^ s)[None] for s in range(mp_parts)], axis=0)

    def to_owners(blocks):
        return [blocks[0]] + [swap(blocks[s], "mp", s) for s in others]

    def by_owner(rows):
        blocks = rows.reshape(mp_parts, -1, rows.shape[1])
        return [pick(blocks, mp_index ^ s) for s in range(mp_parts)]

    def my_part(rows):
        count = rows.shape[0] // dp_parts
        return lax.dynamic_slice_in_dim(rows, dp_index * count, count, 0)

    out_slice = jnp.stack(to_owners([my_part(out_weight)] * mp_parts))
    out_all = jnp.swapaxes(lax.all_gather(out_slice, "dp", axis=0), 0, 1).reshape(width, width)
    bias_row = jnp.pad(up_bias.reshape(1, units), ((0, 15), (0, 0)))
    far_slice = jnp.concatenate([my_part(up_weight), my_part(down_weight), bias_row], axis=0)
    far_slice = swap(far_slice, "mp", 2)
    far_bias = far_slice[-16]

    def project(rows, weight, bias_vec):
        return (dot(rows, weight) + bias_vec.astype(F32)).astype(BF16)

    queries = project(hidden_in, query_weight, query_bias)
    keys_all = project(hidden_in, key_weight, key_bias)
    values_all = project(hidden_in, value_weight, value_bias)
    pos_query = project(position_table, query_weight, query_bias)
    pos_key = project(position_table, key_weight, key_bias)
    row_ids = jnp.arange(position_table.shape[0], dtype=jnp.int32)[None, :]
    falling = jnp.concatenate([bucket_of_offset[:1], bucket_of_offset[::-1]])
    rising = jnp.concatenate([bucket_of_offset, bucket_of_offset[:1]])
    hot_falling = (falling[:, None] == row_ids).astype(BF16)
    hot_rising = (rising[:, None] == row_ids).astype(BF16)
    key_rows = dot(hot_falling, pos_key).astype(BF16)
    query_rows = dot(hot_falling, pos_query).astype(BF16)
    query_rows_up = dot(hot_rising, pos_query).astype(BF16)

    weight_cat = jnp.concatenate([query_weight, key_weight, value_weight], axis=1)

    probs = []
    context = []
    for pair in range(pairs):
        prob, ctx = attn_fwd(
            pair, queries, keys_all, values_all, key_rows, query_rows, key_mask.reshape(1, tokens)
        )
        probs.append(prob)
        context.append(ctx)
        if pair == 0:
            far_all = lax.all_gather(after(far_slice, ctx), "dp", axis=0)
    context = jnp.concatenate(context, axis=1)
    ctx_rows = jnp.concatenate(to_owners(by_owner(context)), axis=1)

    own_rows = lax.dynamic_slice_in_dim(hidden_in, mp_index * share, share, 0)
    pre_first = dot(ctx_rows, out_all) + out_bias.astype(F32) + own_rows.astype(F32)
    unit_first, inverse_first = norm_parts(pre_first)
    gain_first = first_gain.astype(F32)
    normed = unit_first * gain_first + first_shift.astype(F32)
    normed_low = normed.astype(BF16)

    near_low = swap(normed_low, "mp", 1)
    up_cat = jnp.concatenate([up_weight, far_all[:, : width // dp_parts].reshape(width, units)], axis=1)
    down_cat = jnp.concatenate([down_weight, far_all[:, width // dp_parts : -16].reshape(units, width)], axis=0)
    bias_cat = jnp.concatenate([up_bias, far_bias], axis=0).astype(F32)

    def feed(rows):
        act, slope = gelu_parts(dot(rows, up_cat) + bias_cat)
        act_low = act.astype(BF16)
        return act_low, slope.astype(BF16), dot(act_low, down_cat)

    act_near, slope_near, mixed_near = feed(near_low)
    act_own, slope_own, mixed_own = feed(normed_low)
    mixed = mixed_own + swap(mixed_near.astype(BF16), "mp", 1).astype(F32)
    pre_second = mixed + down_bias.astype(F32) + normed

    unit_second, inverse_second = norm_parts(pre_second)
    gain_second = second_gain.astype(F32)
    layer_out = (unit_second * gain_second + second_shift.astype(F32)).astype(BF16)
    cot = cotangent.astype(F32)
    d_pre_second = norm_back(cot, unit_second, inverse_second, gain_second)
    d_down = d_pre_second.astype(BF16)

    near_d_down = swap(d_down, "mp", 1)

    def feed_back(d_rows, slope):
        d_inner = (dot(d_rows, down_cat, NT) * slope.astype(F32)).astype(BF16)
        return d_inner, dot(d_inner, up_cat, NT)

    d_inner_own, back_own = feed_back(d_down, slope_own)
    d_inner_near, back_near = feed_back(near_d_down, slope_near)
    back_near = swap(back_near.astype(BF16), "mp", 1)
    d_normed = back_own + back_near.astype(F32) + d_pre_second
    act_cat = jnp.concatenate([act_own, act_near], axis=0)
    d_down_cat = jnp.concatenate([d_down, near_d_down], axis=0)
    normed_cat = jnp.concatenate([normed_low, near_low], axis=0)
    d_inner_cat = jnp.concatenate([d_inner_own, d_inner_near], axis=0)

    half = dp_parts // 2

    def blocks_of(cols, which, groups):
        step = cols.shape[1] // (groups * dp_parts)
        return jnp.concatenate(
            [
                lax.dynamic_slice_in_dim(cols, (g * dp_parts + 2 * j + which) * step, step, 1)
                for g in range(groups)
                for j in range(half)
            ],
            axis=1,
        )

    def halves_sum(make):
        bit = bit_of("dp", 1)
        theirs = swap(make(1 - bit).astype(BF16), "dp", 1)
        return (make(bit) + theirs.astype(F32)).astype(BF16)

    down_sum = halves_sum(lambda which: dot(blocks_of(act_cat, which, 2), d_down_cat, TN))
    down_sum = down_sum.reshape(2, half, units // dp_parts, width)
    up_sum = halves_sum(lambda which: dot(blocks_of(normed_cat, which, 1), d_inner_cat, TN))
    up_sum = up_sum.reshape(half, width // dp_parts, 2 * units)
    up_bias_part = jnp.sum(d_inner_cat.astype(F32), axis=0)

    d_pre_first = norm_back(d_normed, unit_first, inverse_first, gain_first)
    d_attn = d_pre_first.astype(BF16)
    d_ctx = dot(d_attn, out_all, NT).astype(BF16)
    d_ctx_parts = jnp.stack(
        to_owners([d_ctx[:, s * width_loc : (s + 1) * width_loc] for s in range(mp_parts)])
    )
    out_sum = dot(ctx_rows, d_attn, TN).astype(BF16).reshape(mp_parts, dp_parts, -1, width)
    sums = jnp.stack(
        [
            jnp.sum(d_pre_first, axis=0),
            jnp.sum(d_normed * unit_first, axis=0),
            jnp.sum(d_normed, axis=0),
            jnp.sum(d_pre_second, axis=0),
            jnp.sum(cot * unit_second, axis=0),
            jnp.sum(cot, axis=0),
        ]
    )

    d_ctx = jnp.concatenate(
        [pick(d_ctx_parts, mp_index ^ s) for s in range(mp_parts)], axis=0
    )

    def rows_step(pair, deps):
        return attn_bwd_rows(pair, queries, keys_all, values_all, key_rows, probs[pair], d_ctx, deps)

    def cols_step(pair, deps):
        _, _, _, d_score, turned = by_rows[pair]
        return attn_bwd_cols(pair, keys_all, query_rows_up, d_score, turned, deps)

    low_bits = list(range(len(dp_masks) - 1))
    cut = max(1, len(low_bits) // 2)

    def steps(arrays, ats, bits, left):
        pair = None
        for bit in bits:
            pair = halve(arrays if pair is None else add_all(pair), ats, 1 << left.index(bit), 2 << bit)
            left.remove(bit)
        return pair

    def tied(pair, *deps):
        return pair[0], [after(theirs, *deps) for theirs in pair[1]]

    left_one, left_two = list(low_bits), list(low_bits)
    bits_one, bits_two = low_bits, low_bits[::-1]
    step_two = steps([up_sum], [0], bits_two[:cut], left_two)
    step_out = halve([out_sum], [1], 1, 1)
    step_one = steps([down_sum], [1], bits_one[:cut], left_one)
    by_rows = [rows_step(0, (up_sum, down_sum, step_out[0][0]))]
    (down_sum,) = add_all(tied(step_one, by_rows[0][1]))
    (up_sum,) = add_all(tied(step_two, by_rows[0][1]))
    (out_sum,) = add_all(tied(step_out, by_rows[0][1]))
    step_one = steps([down_sum], [1], bits_one[cut:], left_one)
    step_two = steps([up_sum], [0], bits_two[cut:], left_two)
    step_out = steps([out_sum], [1], bits_one[:cut], list(low_bits))
    by_rows.append(rows_step(1, (by_rows[0][1], down_sum, up_sum, out_sum)))
    d_query, d_value = (jnp.concatenate([r[i] for r in by_rows], axis=1) for i in (0, 1))
    key_grad = jnp.concatenate([r[2] for r in by_rows], axis=0)
    d_value1 = by_rows[1][1]
    (down_sum,) = add_all(tied(step_one, d_value1))
    (up_sum,) = add_all(tied(step_two, d_value1))
    (out_sum,) = add_all(tied(step_out, d_value1))
    step_out = steps([out_sum], [1], bits_one[cut:], low_bits[cut:])
    down_sum, up_sum = down_sum[:, 0], up_sum[0]
    down_rows = down_sum.shape[1]
    far = send_together([down_sum[1], up_sum[:, units:]], "mp", 2)
    by_cols = [cols_step(0, (down_sum, up_sum, out_sum))]
    (out_sum,) = add_all(tied(step_out, by_cols[0][0]))
    out_sum = out_sum[:, 0]
    out_rows = out_sum.shape[1]
    by_cols.append(cols_step(1, (by_cols[0][0], out_sum)))
    d_key = jnp.concatenate([r[0] for r in by_cols], axis=1)
    query_grad = jnp.concatenate([r[1] for r in by_cols], axis=0)
    out_parts = to_owners([out_sum[s] for s in range(mp_parts)])
    out_sum = out_parts[0].astype(F32) + sum(after(p, d_key).astype(F32) for p in out_parts[1:])
    far = [after(part, d_key) for part in far]
    ready = jnp.concatenate(
        [
            add_low(down_sum[0], far[0]),
            add_low(up_sum[:, :units], far[1]),
            out_sum.astype(BF16),
        ],
        axis=0,
    )
    gathered = lax.all_gather(ready, "dp", axis=0)
    d_key1 = after(by_cols[1][0], ready)
    down_weight_grad, up_weight_grad, out_weight_grad = widen(gathered, (down_rows, down_rows, out_rows))

    device_ids = jnp.arange(mp_parts)[:, None]
    up_bias_part = jnp.where(device_ids == mp_index, up_bias_part[:units], 0.0) + jnp.where(
        device_ids == (mp_index ^ 2), up_bias_part[units:], 0.0
    )
    vectors = jnp.concatenate([jnp.zeros_like(up_bias_part), sums, up_bias_part], axis=0)
    vectors = jnp.pad(vectors, ((0, 16 - vectors.shape[0]), (0, 0)))
    message = pack(
        dp_parts,
        mp_index.reshape(1),
        [by_rows[0][0], by_rows[1][0], by_cols[0][0], d_key1, by_rows[0][1], by_rows[1][1]],
        [by_cols[0][1], by_cols[1][1], by_rows[0][2], by_rows[1][2]],
        hidden_in,
        position_table,
        rising[None, :],
        falling[None, :],
        vectors,
    )

    (message,) = add_all(halve([message], [0], 1, 1))
    block_index = dp_index // 2
    total = pick(message, block_index).astype(F32)
    for s in range(1, half):
        total = total + swap(pick(message, block_index ^ s), "dp", 2 * s).astype(F32)
    step = 3 * width_loc // dp_parts
    table_rows = position_table.shape[0]
    table_step = table_rows // dp_parts
    packed = total[up_16(step) : up_16(step) + table_step // 2].astype(BF16)
    packed = jnp.concatenate([packed[:, : 2 * width_loc], packed[:, 2 * width_loc :]], axis=0)
    table_part = dot(packed, weight_cat[:, : 2 * width_loc], NT)
    shared_sum = jnp.concatenate([to_16(table_part), total[-16:]], axis=0).astype(BF16)
    shared_sum = low_sum_over(shared_sum, "mp")
    block = jnp.concatenate([total[: up_16(step)].astype(BF16), shared_sum], axis=0)
    d_cat = after(jnp.concatenate([d_query, d_key, d_value], axis=1), shared_sum, gathered)
    input_part = dot(d_cat, weight_cat, NT).astype(BF16)
    input_part = lax.psum_scatter(input_part, "mp", scatter_dimension=0, tiled=True)
    input_grad = d_pre_first + input_part.astype(F32)

    parts = jnp.stack([block] + [swap(block, "dp", 2 * s) for s in range(1, half)])
    mine = jnp.stack([pick(parts, block_index ^ j) for j in range(half)])
    mine = after(mine, down_weight_grad)
    theirs = swap(mine, "dp", 1)
    even = bit_of("dp", 1) == 0
    whole = jnp.stack([jnp.where(even, mine, theirs), jnp.where(even, theirs, mine)], axis=1)
    whole = whole.reshape(dp_parts, -1, width)
    query_weight_grad, key_weight_grad, value_weight_grad, table_grad, vectors = unpack(
        whole, width_loc, table_rows
    )
    biases = lax.dynamic_index_in_dim(vectors, mp_index, 0, keepdims=False)
    query_bias_grad, key_bias_grad, value_bias_grad = (
        biases[i * width_loc : (i + 1) * width_loc] for i in range(3)
    )
    shared_sums = vectors[mp_parts:]
    up_bias_grad = lax.dynamic_index_in_dim(vectors, mp_parts + 6 + mp_index, 0, keepdims=False)

    out_bias_grad, first_gain_grad, first_shift_grad, down_bias_grad, second_gain_grad, second_shift_grad = (
        shared_sums[i] for i in range(6)
    )
    return (
        layer_out,
        input_grad,
        table_grad,
        query_weight_grad,
        query_bias_grad,
        key_weight_grad,
        key_bias_grad,
        value_weight_grad,
        value_bias_grad,
        out_weight_grad,
        out_bias_grad,
        first_gain_grad,
        first_shift_grad,
        up_weight_grad,
        up_bias_grad,
        down_weight_grad,
        down_bias_grad,
        second_gain_grad,
        second_shift_grad,
    )


def solution(mesh):
    return jax.shard_map(
        on_device,
        mesh=mesh,
        in_specs=(
            P("dp", None),
            P("dp"),
            P(),
            P(),
            P(None, "mp"),
            P("mp"),
            P(None, "mp"),
            P("mp"),
            P(None, "mp"),
            P("mp"),
            P("mp", None),
            P(),
            P(),
            P(),
            P(None, "mp"),
            P("mp"),
            P("mp", None),
            P(),
            P(),
            P(),
            P(("dp", "mp"), None),
        ),
        out_specs=(
            P(("dp", "mp"), None),
            P(("dp", "mp"), None),
            P(),
            P(None, "mp"),
            P("mp"),
            P(None, "mp"),
            P("mp"),
            P(None, "mp"),
            P("mp"),
            P("mp", None),
            P(),
            P(),
            P(),
            P(None, "mp"),
            P("mp"),
            P("mp", None),
            P(),
            P(),
            P(),
        ),
        check_vma=False,
    )
```

time: 4200 us -> 390 us (0.09)
  other arithmetic: 2260 us -> 28.6 us
  local copies, waits for them, and re-layouts: 998 us -> 26.1 us
  waiting for transfers between devices: 562 us -> 114 us
  matrix products: 271 us -> 46.9 us
  Pallas kernels: 0 us -> 102 us
  blocking collectives: 54.1 us -> 0 us
  starting transfers between devices: 0.84 us -> 50.3 us
    select_n x106 -> x0, other arithmetic: 1550 us -> none  [shear_rows(): current = jnp.where(chosen, moved, current)]
    slice x103 -> x11, local copies, waits for them, and re-layouts: 811 us -> 5.45 us  [the longest x1 2.85 us: on_device(): far_all[:, width // dp_parts:-16].reshape(units, width)]
    add_any x34 -> x0, other arithmetic: 531 us -> none  [shear_rows(): moved = jnp.concatenate([current[..., step_size:], filler], axis=-1)]
    reduce_scatter x4 -> x1, waiting for transfers between devices: 260 us -> 11.5 us  [on_device(): lax.psum_scatter(input_part, 'mp', scatter_dimension=0, tiled=True)]
    dot_general x62 -> x24, matrix products: 271 us -> 46.9 us  [dot(): return lax.dot_general(left, right, dims, preferred_element_type=F32)]
    psum x2 -> x0, waiting for transfers between devices: 172 us -> none  [the longest x1 137 us: on_device(): lax.psum((table_grad, out_bias_grad, first_gain_grad, first_shift_grad, d...]
    while x350 -> x0, local copies, waits for them, and re-layouts: 157 us -> none
    all_gather x3, waiting for transfers between devices: 129 us -> 0.02 us  [the longest x1 0.02 us: on_device(): gathered = lax.all_gather(ready, 'dp', axis=0)]
  transfers between devices with their start and end apart: 9 -> 41, of which waited for: 9 -> 21; matrix products, arithmetic and copies ran while one was open for 1% -> 16% of each run, Pallas kernels for 0% -> 27%
where the time goes in v2:
time: 390 us; the launch traced here: 383 us
  waiting for transfers between devices  114 us (29%)
  Pallas kernels  102 us (26%)
  starting transfers between devices  50.3 us (13%)
  matrix products  46.9 us (12%)
  other arithmetic  28.6 us (7%)
  local copies, waits for them, and re-layouts  26.1 us (7%)
  between operations  15.6 us (4%)
    ppermute x37, waiting for transfers between devices, swap(): lax.ppermute(values, axis, [(i, i ^ mask) for i in range(lax.axis_size(ax...  102 us
    ppermute x37, starting transfers between devices, swap(): lax.ppermute(values, axis, [(i, i ^ mask) for i in range(lax.axis_size(ax...  49.8 us
    dot_general x24, matrix products, dot(): return lax.dot_general(left, right, dims, preferred_element_type=F32)  46.9 us
    pallas_call x2, Pallas kernels, attn_fwd(): pl.pallas_call(ordered(fwd_kernel, 6, deps), grid=(length // BLK,), in_sp...  32.7 us
    pallas_call x2, Pallas kernels, attn_bwd_rows(): pl.pallas_call(ordered(bwd_rows_kernel, 6, deps), grid=(steps,), in_specs...  31.3 us
    pallas_call x2, Pallas kernels, attn_bwd_cols(): pl.pallas_call(ordered(bwd_cols_kernel, 4, deps), grid=(length // BLK,),...  20.1 us
    unnamed x164, local copies, waits for them, and re-layouts  12.7 us
    reduce_scatter x1, waiting for transfers between devices, on_device(): lax.psum_scatter(input_part, 'mp', scatter_dimension=0, tiled=True)  11.5 us
  transfers between devices with their start and end apart: 41, of which 21 were waited for; matrix products, arithmetic and copies ran while one was open for 16% of the time, Pallas kernels for 27%

profile of v2, /device:TPU:0, one launch (start us, length us, event | category | flops | bytes accessed | tf_op | source)
XLA Modules:
  0.0 383.3 jit_solution(8749908986827394621)
XLA Ops:
  8.2 3.0 collective-permute-start.3
  11.3 2.6 collective-permute-start.4
  14.6 4.0 %collective-permute-done.4 = bf16[32,1024]{1,0:T(8,128)(2,1)S(1)} collective-permute-done((bf16[32,1024]{1,0:T(8,128)(2,1)S(1)}, bf16[32,1024]{1,0:T(8,128)(2,1)S(1)}, u32[]{:S(2)}, u32[]{:S(2)}) %collective-permute-start.4) | collective-permute-done | bytes 65568 | tf_op jit(solution)/shard_map/ppermute | solution.py:396
  22.7 1.6 collective-permute-start.6
  26.8 1.8 fusion.5.refs_4_
  28.7 1.6 fusion.4.refs_3_
  30.3 2.5 fusion.34.refs_1_.refs_0_
  35.4 16.4 %attn_fwd.2 = (bf16[2,1024,1024]{2,1,0:T(8,128)(2,1)}, bf16[1024,128]{1,0:T(8,128)(2,1)S(1)}) custom-call(bf16[1024,256]{1,0:T(8,128)(2,1)S(1)} %fusion.33.refs_0_, bf16[1024,256]{1,0:T(8,128)(2,1)S(1)} %fusion.34.refs_1_.refs_0_, bf16[1024,256]{1,0:T(8,128)(2,1)S(1)} %fusion.35.refs_2_, bf16[2048,256]{1,0:T(8,128)(2,1)S(1)} %fusion.4.refs_3_, ...), custom_call_target="tpu_custom_call" | custom-call | flops 17179869184 | bytes 10485760 | tf_op jit(solution)/shard_map/attn_fwd/pallas_call | solution.py:107
  53.2 16.4 %attn_fwd.3 = (bf16[2,1024,1024]{2,1,0:T(8,128)(2,1)}, bf16[1024,128]{1,0:T(8,128)(2,1)S(1)}) custom-call(bf16[1024,256]{1,0:T(8,128)(2,1)S(1)} %fusion.33.refs_0_, bf16[1024,256]{1,0:T(8,128)(2,1)S(1)} %fusion.34.refs_1_.refs_0_, bf16[1024,256]{1,0:T(8,128)(2,1)S(1)} %fusion.35.refs_2_, bf16[2048,256]{1,0:T(8,128)(2,1)S(1)} %fusion.4.refs_3_, ...), custom_call_target="tpu_custom_call" | custom-call | flops 17179869184 | bytes 10485760 | tf_op jit(solution)/shard_map/attn_fwd/pallas_call | solution.py:107
  71.2 3.0 collective-permute-start.2
  75.5 1.8 copy.68
  77.3 4.3 %collective-permute-done.1 = bf16[256,256]{1,0:T(8,128)(2,1)S(1)} collective-permute-done((bf16[256,256]{1,0:T(8,128)(2,1)S(1)}, bf16[256,256]{1,0:T(8,128)(2,1)S(1)}, u32[]{:S(2)}, u32[]{:S(2)}) %collective-permute-start.1) | collective-permute-done | bytes 131104 | tf_op jit(solution)/shard_map/ppermute | solution.py:396
  82.3 2.0 fusion.136
  85.6 2.0 collective-permute-start.7
  90.8 2.8 fusion.3.refs_1_
  95.0 3.6 collective-permute-done.7
  98.6 1.6 fusion.111
  100.2 2.1 fusion.105
  102.3 2.8 fusion.130
  105.2 2.6 multiply_convert_fusion.1
  107.8 2.7 multiply_convert_fusion
  111.8 1.8 collective-permute-start.8
  114.3 9.3 %collective-permute-done.8 = bf16[256,1024]{1,0:T(8,128)(2,1)S(1)} collective-permute-done((bf16[256,1024]{1,0:T(8,128)(2,1)S(1)}, bf16[256,1024]{1,0:T(8,128)(2,1)S(1)}, u32[]{:S(2)}, u32[]{:S(2)}) %collective-permute-start.8) | collective-permute-done | bytes 524320 | tf_op jit(solution)/shard_map/ppermute | solution.py:396
  123.7 1.5 fusion.137
  126.5 1.8 fusion.127
  128.5 1.6 collective-permute-start.9
  130.4 9.0 %collective-permute-done.9 = bf16[256,1024]{1,0:T(8,128)(2,1)S(1)} collective-permute-done((bf16[256,1024]{1,0:T(8,128)(2,1)S(1)}, bf16[256,1024]{1,0:T(8,128)(2,1)S(1)}, u32[]{:S(2)}, u32[]{:S(2)}) %collective-permute-start.9) | collective-permute-done | bytes 524320 | tf_op jit(solution)/shard_map/ppermute | solution.py:396
  139.4 4.9 %fusion.7 = bf16[256,2048]{1,0:T(8,128)(2,1)S(1)} fusion(bf16[256,1024]{1,0:T(8,128)(2,1)S(1)} %collective-permute-done.9, f32[256,2048]{1,0:T(8,128)S(1)} %get-tuple-element.180, bf16[1024,1024]{1,0:T(8,128)(2,1)S(1)} %bitcast.203, bf16[1024,1024]{1,0:T(8,128)(2,1)S(1)} %copy-done.44), kind=kOutput, calls=%fused_computation.54 | convolution fusion | flops 1088421888 | bytes 7864320 | tf_op jit(solution)/shard_map/dot_general | solution.py:29
  147.1 4.5 %fusion.6 = bf16[256,2048]{1,0:T(8,128)(2,1)S(1)} fusion(bf16[256,1024]{1,0:T(8,128)(2,1)S(1)} %convert_element_type.346, f32[256,2048]{1,0:T(8,128)S(1)} %get-tuple-element.182, bf16[1024,1024]{1,0:T(8,128)(2,1)S(1)} %bitcast.204, bf16[1024,1024]{1,0:T(8,128)(2,1)S(1)} %copy-done.44), kind=kOutput, calls=%fused_computation.53 | convolution fusion | flops 1088421888 | bytes 7864320 | tf_op jit(solution)/shard_map/dot_general | solution.py:29
  155.7 2.3 multiply_reduce_fusion
  161.5 1.8 collective-permute-start.12
  163.3 1.5 collective-permute-start.13
  166.7 6.7 %collective-permute-done.12 = bf16[256,256]{1,0:T(8,128)(2,1)S(1)} collective-permute-done((bf16[256,256]{1,0:T(8,128)(2,1)S(1)}, bf16[256,256]{1,0:T(8,128)(2,1)S(1)}, u32[]{:S(2)}, u32[]{:S(2)}) %collective-permute-start.12) | collective-permute-done | bytes 131104 | tf_op jit(solution)/shard_map/ppermute | solution.py:396
  175.1 1.5 collective-permute-start.17
  178.1 1.5 collective-permute-start.16
  179.6 15.8 %attn_bwd_rows.2 = (bf16[1024,128]{1,0:T(8,128)(2,1)S(1)}, bf16[1024,128]{1,0:T(8,128)(2,1)S(1)}, bf16[128,2048]{1,0:T(8,128)(2,1)S(1)}, bf16[2,1024,1024]{2,1,0:T(8,128)(2,1)}, bf16[1024,128]{1,0:T(8,128)(2,1)S(1)}) custom-call(bf16[1024,256]{1,0:T(8,128)(2,1)S(1)} %fusion.33.refs_0_, bf16[1024,256]{1,0:T(8,128)(2,1)S(1)} %fusion.34.refs_1_.refs_0_, ...), custom_call_target="tpu_custom_call" | custom-call | flops 17179869184 | bytes 10485760 | tf_op jit(solution)/shard_map/attn_bwd_rows/pallas_call | solution.py:183
  198.6 4.4 %collective-permute-done.16 = bf16[512,1024]{1,0:T(8,128)(2,1)S(1)} collective-permute-done((bf16[512,1024]{1,0:T(8,128)(2,1)S(1)}, bf16[512,1024]{1,0:T(8,128)(2,1)S(1)}, u32[]{:S(2)}, u32[]{:S(2)}) %collective-permute-start.16) | collective-permute-done | bytes 1048608 | tf_op jit(solution)/shard_map/ppermute | solution.py:396
  203.9 1.6 collective-permute-start.20
  205.4 15.6 %attn_bwd_rows.3 = (bf16[1024,128]{1,0:T(8,128)(2,1)S(1)}, bf16[1024,128]{1,0:T(8,128)(2,1)S(1)}, bf16[128,2048]{1,0:T(8,128)(2,1)S(1)}, bf16[2,1024,1024]{2,1,0:T(8,128)(2,1)}, bf16[1024,128]{1,0:T(8,128)(2,1)S(1)}) custom-call(bf16[1024,256]{1,0:T(8,128)(2,1)S(1)} %copy-done.8, bf16[1024,256]{1,0:T(8,128)(2,1)S(1)} %fusion.34.refs_1_.refs_0_, ...), custom_call_target="tpu_custom_call" | custom-call | flops 17179869184 | bytes 10485760 | tf_op jit(solution)/shard_map/attn_bwd_rows/pallas_call | solution.py:183
  224.4 5.9 %collective-permute-done.19 = bf16[256,1024]{1,0:T(8,128)(2,1)S(1)} collective-permute-done((bf16[256,1024]{1,0:T(8,128)(2,1)S(1)}, bf16[256,1024]{1,0:T(8,128)(2,1)S(1)}, u32[]{:S(2)}, u32[]{:S(2)}) %collective-permute-start.19) | collective-permute-done | bytes 524320 | tf_op jit(solution)/shard_map/ppermute | solution.py:396
  230.6 5.6 %collective-permute-start.23 = (bf16[256,1024]{1,0:T(8,128)(2,1)S(1)}, bf16[256,1024]{1,0:T(8,128)(2,1)S(1)}, u32[]{:S(2)}, u32[]{:S(2)}) collective-permute-start(bf16[256,1024]{1,0:T(8,128)(2,1)S(1)} %pad_maximum_fusion.18), channel_id=1, source_target_pairs={{0,2},{1,3},{2,0},{3,1},{4,6},{5,7},{6,4},{7,5},{8,10},{9,11},{10,... | collective-permute-start | bytes 1572872 | tf_op jit(solution)/shard_map/ppermute | solution.py:396
  236.2 10.0 %attn_bwd_cols.2 = (bf16[1024,128]{1,0:T(8,128)(2,1)S(1)}, bf16[128,2048]{1,0:T(8,128)(2,1)S(1)}) custom-call(bf16[1024,256]{1,0:T(8,128)(2,1)S(1)} %fusion.34.refs_1_.refs_0_, bf16[2048,256]{1,0:T(8,128)(2,1)S(1)} %copy-done.11, bf16[2,1024,1024]{2,1,0:T(8,128)(2,1)S(1)} %copy-done.14, bf16[1024,128]{1,0:T(8,128)(2,1)S(1)} %get-tuple-element.73.refs_3_, ...), custom_call_target="tpu_custom_call" | custom-call | flops 11811160064 | bytes 10485760 | tf_op jit(solution)/shard_map/attn_bwd_cols/pallas_call | solution.py:249
  246.8 2.9 collective-permute-start.25
  250.9 10.0 %attn_bwd_cols.3 = (bf16[1024,128]{1,0:T(8,128)(2,1)S(1)}, bf16[128,2048]{1,0:T(8,128)(2,1)S(1)}) custom-call(bf16[1024,256]{1,0:T(8,128)(2,1)S(1)} %fusion.34.refs_1_.refs_0_, bf16[2048,256]{1,0:T(8,128)(2,1)S(1)} %copy-done.11, bf16[2,1024,1024]{2,1,0:T(8,128)(2,1)S(1)} %copy-done.15, bf16[1024,128]{1,0:T(8,128)(2,1)S(1)} %get-tuple-element.80.refs_3_, ...), custom_call_target="tpu_custom_call" | custom-call | flops 11811160064 | bytes 10485760 | tf_op jit(solution)/shard_map/attn_bwd_cols/pallas_call | solution.py:249
  264.1 1.9 convert_reduce_fusion
  269.5 7.7 %pack.1 = bf16[8,144,1024]{2,1,0:T(8,128)(2,1)} custom-call(s32[1]{0:T(128)} %bitcast.51.refs_0_, bf16[1024,128]{1,0:T(8,128)(2,1)S(1)} %get-tuple-element.65.refs_1_, bf16[1024,128]{1,0:T(8,128)(2,1)S(1)} %get-tuple-element.71.refs_2_, bf16[1024,128]{1,0:T(8,128)(2,1)S(1)} %get-tuple-element.78.refs_4_.refs_3_, ...), custom_call_target="tpu_custom_call" | custom-call | flops 8000000000 | bytes 10485760 | tf_op jit(solution)/shard_map/pack/pallas_call | solution.py:335
  278.6 2.8 collective-permute-done.27
  281.5 1.7 fusion.8
  286.8 10.9 %collective-permute-done.28 = bf16[144,1024]{1,0:T(8,128)(2,1)S(1)} collective-permute-done((bf16[144,1024]{1,0:T(8,128)(2,1)S(1)}, bf16[144,1024]{1,0:T(8,128)(2,1)S(1)}, u32[]{:S(2)}, u32[]{:S(2)}) %collective-permute-start.28) | collective-permute-done | bytes 294944 | tf_op jit(solution)/shard_map/ppermute | solution.py:396
  297.7 4.6 %collective-permute-done.29 = bf16[144,1024]{1,0:T(8,128)(2,1)S(1)} collective-permute-done((bf16[144,1024]{1,0:T(8,128)(2,1)S(1)}, bf16[144,1024]{1,0:T(8,128)(2,1)S(1)}, u32[]{:S(2)}, u32[]{:S(2)}) %collective-permute-start.29) | collective-permute-done | bytes 294944 | tf_op jit(solution)/shard_map/ppermute | solution.py:396
  302.3 7.6 %collective-permute-done.30 = bf16[144,1024]{1,0:T(8,128)(2,1)} collective-permute-done((bf16[144,1024]{1,0:T(8,128)(2,1)S(1)}, bf16[144,1024]{1,0:T(8,128)(2,1)}, u32[]{:S(2)}, u32[]{:S(2)}) %collective-permute-start.30) | collective-permute-done | bytes 294944 | tf_op jit(solution)/shard_map/ppermute | solution.py:396
  311.2 1.8 convolution_convert_fusion.7
  313.1 5.3 %collective-permute-done.31 = bf16[80,1024]{1,0:T(8,128)(2,1)S(1)} collective-permute-done((bf16[80,1024]{1,0:T(8,128)(2,1)S(1)}, bf16[80,1024]{1,0:T(8,128)(2,1)S(1)}, u32[]{:S(2)}, u32[]{:S(2)}) %collective-permute-start.31) | collective-permute-done | bytes 163872 | tf_op jit(solution)/shard_map/ppermute | solution.py:396
  320.4 5.6 %collective-permute-done.32 = bf16[80,1024]{1,0:T(8,128)(2,1)S(1)} collective-permute-done((bf16[80,1024]{1,0:T(8,128)(2,1)S(1)}, bf16[80,1024]{1,0:T(8,128)(2,1)S(1)}, u32[]{:S(2)}, u32[]{:S(2)}) %collective-permute-start.32) | collective-permute-done | bytes 163872 | tf_op jit(solution)/shard_map/ppermute | solution.py:396
  326.0 4.6 %convolution_convert_fusion.3 = bf16[1024,1024]{1,0:T(8,128)(2,1)} fusion(bf16[1024,768]{1,0:T(8,128)(2,1)} %constant_dynamic-update-slice_fusion, bf16[1024,256]{1,0:T(8,128)(2,1)S(1)} %copy-done.72, bf16[1024,256]{1,0:T(8,128)(2,1)S(1)} %copy-done.70, bf16[1024,256]{1,0:T(8,128)(2,1)S(1)} %copy-done.68), kind=kOutput, calls=%fused_computation.98 | convolution fusion | flops 1616379904 | bytes 5242880 | tf_op jit(solution)/shard_map/dot_general | solution.py:29
  330.7 2.6 collective-permute-start.33
  333.3 1.5 collective-permute-start.34
  334.9 6.6 %collective-permute-done.33 = bf16[176,1024]{1,0:T(8,128)(2,1)S(1)} collective-permute-done((bf16[176,1024]{1,0:T(8,128)(2,1)S(1)}, bf16[176,1024]{1,0:T(8,128)(2,1)S(1)}, u32[]{:S(2)}, u32[]{:S(2)}) %collective-permute-start.33) | collective-permute-done | bytes 360480 | tf_op jit(solution)/shard_map/ppermute | solution.py:396
  341.5 5.3 %collective-permute-done.34 = bf16[176,1024]{1,0:T(8,128)(2,1)S(1)} collective-permute-done((bf16[176,1024]{1,0:T(8,128)(2,1)S(1)}, bf16[176,1024]{1,0:T(8,128)(2,1)S(1)}, u32[]{:S(2)}, u32[]{:S(2)}) %collective-permute-start.34) | collective-permute-done | bytes 360480 | tf_op jit(solution)/shard_map/ppermute | solution.py:396
  347.3 7.5 %widen.1 = (f32[1024,1024]{1,0:T(8,128)}, f32[1024,1024]{1,0:T(8,128)}, f32[256,1024]{1,0:T(8,128)}) custom-call(bf16[8,288,1024]{2,1,0:T(8,128)(2,1)} %bitcast.191), custom_call_target="tpu_custom_call" | custom-call | bytes 14155776 | tf_op jit(solution)/shard_map/widen/pallas_call | solution.py:384
  354.8 3.2 collective-permute-done.36
  359.0 2.6 unpack.1
  362.8 11.5 %reduce-scatter.2.cloned.1.call-done = bf16[256,1024]{1,0:T(8,128)(2,1)} async-done(((bf16[1024,1024]{1,0:T(8,128)(2,1)}), bf16[256,1024]{1,0:T(8,128)(2,1)}) %reduce-scatter.2.cloned.1.call-update) | async-done | bytes 524304 | tf_op jit(solution)/shard_map/reduce_scatter | solution.py:751
  374.4 2.1 convert_add_fusion.4
  (333 shorter events, 67.3 us)
Async XLA Ops:
  7.2 17.0 %copy-start.43 = (s32[2047]{0:T(1024)S(1)}, s32[2047]{0:T(1024)}, u32[]{:S(2)}) copy-start(s32[2047]{0:T(1024)} %param.23) | copy-start | bytes 24568
  7.2 17.7 %copy-start.75 = (bf16[256]{0:T(256)(128)(2,1)S(1)}, bf16[256]{0:T(256)(128)(2,1)}, u32[]{:S(2)}) copy-start(bf16[256]{0:T(256)(128)(2,1)} %param.28) | copy-start | bytes 1540
  7.2 17.7 %copy-start.76 = (bf16[256]{0:T(256)(128)(2,1)S(1)}, bf16[256]{0:T(256)(128)(2,1)}, u32[]{:S(2)}) copy-start(bf16[256]{0:T(256)(128)(2,1)} %param.26) | copy-start | bytes 1540
  7.2 17.7 %copy-start.77 = (bf16[256]{0:T(256)(128)(2,1)S(1)}, bf16[256]{0:T(256)(128)(2,1)}, u32[]{:S(2)}) copy-start(bf16[256]{0:T(256)(128)(2,1)} %param.30) | copy-start | bytes 1540
  7.2 18.4 %copy-start.4 = (bf16[512,1024]{1,0:T(8,128)(2,1)S(1)}, bf16[512,1024]{1,0:T(8,128)(2,1)}, u32[]{:S(2)}) copy-start(bf16[512,1024]{1,0:T(8,128)(2,1)} %refs_12_.1) | copy-start | bytes 3145732
  7.3 18.4 %copy-start.66 = (bf16[1024,256]{1,0:T(8,128)(2,1)S(1)}, bf16[1024,256]{1,0:T(8,128)(2,1)}, u32[]{:S(2)}) copy-start(bf16[1024,256]{1,0:T(8,128)(2,1)} %param.25) | copy-start | bytes 1572868
  7.3 68.2 %all-gather.7.cloned.1.call-start = ((), (), s32[]{:S(2)}) async-start(), calls=%async_computation.2 | async-start | bytes 2359296 | tf_op jit(solution)/shard_map/all_gather | solution.py:524
  8.2 6.3 %collective-permute-start.3 = (bf16[32,1024]{1,0:T(8,128)(2,1)S(1)}, bf16[32,1024]{1,0:T(8,128)(2,1)S(1)}, u32[]{:S(2)}, u32[]{:S(2)}) collective-permute-start(bf16[32,1024]{1,0:T(8,128)(2,1)S(1)} %constant_dynamic-slice_fusion.16), channel_id=1, source_target_pairs={{0,1},{1,0},{2,3},{3,2},{4,5},{5,4},{6,7},{7,6},{8,9},{9,8},{10,11... | collective-permute-start | bytes 196616 | tf_op jit(solution)/shard_map/ppermute | solution.py:396
  11.3 7.3 %collective-permute-start.4 = (bf16[32,1024]{1,0:T(8,128)(2,1)S(1)}, bf16[32,1024]{1,0:T(8,128)(2,1)S(1)}, u32[]{:S(2)}, u32[]{:S(2)}) collective-permute-start(bf16[32,1024]{1,0:T(8,128)(2,1)S(1)} %constant_dynamic-slice_fusion.16), channel_id=1, source_target_pairs={{0,2},{1,3},{2,0},{3,1},{4,6},{5,7},{6,4},{7,5},{8,10},{9,11},{10,... | collective-permute-start | bytes 196616 | tf_op jit(solution)/shard_map/ppermute | solution.py:396
  13.9 6.1 %collective-permute-start.5 = (bf16[32,1024]{1,0:T(8,128)(2,1)S(1)}, bf16[32,1024]{1,0:T(8,128)(2,1)S(1)}, u32[]{:S(2)}, u32[]{:S(2)}) collective-permute-start(bf16[32,1024]{1,0:T(8,128)(2,1)S(1)} %constant_dynamic-slice_fusion.16), channel_id=1, source_target_pairs={{0,3},{1,2},{2,1},{3,0},{4,7},{5,6},{6,5},{7,4},{8,11},{9,10},{10,... | collective-permute-start | bytes 196616 | tf_op jit(solution)/shard_map/ppermute | solution.py:396
  20.7 81.6 %all-gather.9.cloned.1.call-start = ((), (), s32[]{:S(2)}) async-start(), calls=%async_computation.3 | async-start | bytes 5013504 | tf_op jit(solution)/shard_map/all_gather | solution.py:558
  22.7 29.0 %collective-permute-start.6 = (bf16[272,1024]{1,0:T(8,128)(2,1)}, bf16[272,1024]{1,0:T(8,128)(2,1)}, u32[]{:S(2)}, u32[]{:S(2)}) collective-permute-start(bf16[272,1024]{1,0:T(8,128)(2,1)} %fusion.52), channel_id=1, source_target_pairs={{0,2},{1,3},{2,0},{3,1},{4,6},{5,7},{6,4},{7,5},{8,10},{9,11},{10,... | collective-permute-start | bytes 1671176 | tf_op jit(solution)/shard_map/ppermute | solution.py:396
  33.9 145.7 %copy-start.7 = (bf16[1024,256]{1,0:T(8,128)(2,1)}, bf16[1024,256]{1,0:T(8,128)(2,1)S(1)}, u32[]{:S(2)}) copy-start(bf16[1024,256]{1,0:T(8,128)(2,1)S(1)} %fusion.33.refs_0_) | copy-start | bytes 1572868
  34.6 17.3 %copy-start.9 = (bf16[1024,256]{1,0:T(8,128)(2,1)}, bf16[1024,256]{1,0:T(8,128)(2,1)S(1)}, u32[]{:S(2)}) copy-start(bf16[1024,256]{1,0:T(8,128)(2,1)S(1)} %fusion.35.refs_2_) | copy-start | bytes 1572868
  51.7 274.2 %all-gather.11.cloned.1.call-start = ((), (), s32[]{:S(2)}) async-start(), calls=%async_computation.4 | async-start | bytes 5308416 | tf_op jit(solution)/shard_map/all_gather | solution.py:713
  69.7 7.5 %collective-permute-start = (bf16[256,256]{1,0:T(8,128)(2,1)S(1)}, bf16[256,256]{1,0:T(8,128)(2,1)S(1)}, u32[]{:S(2)}, u32[]{:S(2)}) collective-permute-start(bf16[256,256]{1,0:T(8,128)(2,1)S(1)} %get-tuple-element.154), channel_id=1, source_target_pairs={{0,1},{1,0},{2,3},{3,2},{4,5},{5,4},{6,7},{7,6},{8,9},{9,8},{10,11... | collective-permute-start | bytes 393224 | tf_op jit(solution)/shard_map/ppermute | solution.py:396
  70.5 11.1 %collective-permute-start.1 = (bf16[256,256]{1,0:T(8,128)(2,1)S(1)}, bf16[256,256]{1,0:T(8,128)(2,1)S(1)}, u32[]{:S(2)}, u32[]{:S(2)}) collective-permute-start(bf16[256,256]{1,0:T(8,128)(2,1)S(1)} %get-tuple-element.153), channel_id=1, source_target_pairs={{0,2},{1,3},{2,0},{3,1},{4,6},{5,7},{6,4},{7,5},{8,10},{9,11},{10,... | collective-permute-start | bytes 393224 | tf_op jit(solution)/shard_map/ppermute | solution.py:396
  71.2 10.4 %collective-permute-start.2 = (bf16[256,256]{1,0:T(8,128)(2,1)S(1)}, bf16[256,256]{1,0:T(8,128)(2,1)S(1)}, u32[]{:S(2)}, u32[]{:S(2)}) collective-permute-start(bf16[256,256]{1,0:T(8,128)(2,1)S(1)} %get-tuple-element.152), channel_id=1, source_target_pairs={{0,3},{1,2},{2,1},{3,0},{4,7},{5,6},{6,5},{7,4},{8,11},{9,10},{10,... | collective-permute-start | bytes 393224 | tf_op jit(solution)/shard_map/ppermute | solution.py:396
  85.6 13.0 %collective-permute-start.7 = (bf16[256,1024]{1,0:T(8,128)(2,1)}, bf16[256,1024]{1,0:T(8,128)(2,1)}, u32[]{:S(2)}, u32[]{:S(2)}) collective-permute-start(bf16[256,1024]{1,0:T(8,128)(2,1)} %fusion.47), channel_id=1, source_target_pairs={{0,1},{1,0},{2,3},{3,2},{4,5},{5,4},{6,7},{7,6},{8,9},{9,8},{10,11... | collective-permute-start | bytes 1572872 | tf_op jit(solution)/shard_map/ppermute | solution.py:396
  111.8 11.8 %collective-permute-start.8 = (bf16[256,1024]{1,0:T(8,128)(2,1)S(1)}, bf16[256,1024]{1,0:T(8,128)(2,1)S(1)}, u32[]{:S(2)}, u32[]{:S(2)}) collective-permute-start(bf16[256,1024]{1,0:T(8,128)(2,1)S(1)} %convolution_convert_fusion.6), channel_id=1, source_target_pairs={{0,1},{1,0},{2,3},{3,2},{4,5},{5,4},{6,7},{7,6},{8,9},{9,8},{10,11... | collective-permute-start | bytes 1572872 | tf_op jit(solution)/shard_map/ppermute | solution.py:396
  114.1 9.5 %copy-start.51 = (f32[1024]{0:T(1024)S(1)}, f32[1024]{0:T(1024)}, u32[]{:S(2)}) copy-start(f32[1024]{0:T(1024)} %copy-done.50) | copy-start | bytes 12292
  114.2 9.5 %copy-start.54 = (f32[256]{0:T(256)S(1)}, f32[256]{0:T(256)}, u32[]{:S(2)}) copy-start(f32[256]{0:T(256)} %copy-done.53) | copy-start | bytes 3076
  114.3 11.1 %copy-start.30 = (bf16[256,1024]{1,0:T(8,128)(2,1)S(1)}, bf16[256,1024]{1,0:T(8,128)(2,1)}, u32[]{:S(2)}) copy-start(bf16[256,1024]{1,0:T(8,128)(2,1)} %param.41) | copy-start | bytes 1572868
  128.5 10.9 %collective-permute-start.9 = (bf16[256,1024]{1,0:T(8,128)(2,1)S(1)}, bf16[256,1024]{1,0:T(8,128)(2,1)S(1)}, u32[]{:S(2)}, u32[]{:S(2)}) collective-permute-start(bf16[256,1024]{1,0:T(8,128)(2,1)S(1)} %convert_element_type.346), channel_id=1, source_target_pairs={{0,1},{1,0},{2,3},{3,2},{4,5},{5,4},{6,7},{7,6},{8,9},{9,8},{10,11... | collective-permute-start | bytes 1572872 | tf_op jit(solution)/shard_map/ppermute | solution.py:396
  139.4 12.3 %copy-start.73 = (bf16[256,1024]{1,0:T(8,128)(2,1)}, bf16[256,1024]{1,0:T(8,128)(2,1)S(1)}, u32[]{:S(2)}) copy-start(bf16[256,1024]{1,0:T(8,128)(2,1)S(1)} %collective-permute-done.9) | copy-start | bytes 1572868
  144.3 29.3 %copy-start.31 = (bf16[256,2048]{1,0:T(8,128)(2,1)}, bf16[256,2048]{1,0:T(8,128)(2,1)S(1)}, u32[]{:S(2)}) copy-start(bf16[256,2048]{1,0:T(8,128)(2,1)S(1)} %fusion.7) | copy-start | bytes 3145732
  145.7 10.0 %collective-permute-start.10 = (bf16[256,1024]{1,0:T(8,128)(2,1)S(1)}, bf16[256,1024]{1,0:T(8,128)(2,1)S(1)}, u32[]{:S(2)}, u32[]{:S(2)}) collective-permute-start(bf16[256,1024]{1,0:T(8,128)(2,1)S(1)} %convolution_convert_fusion.5), channel_id=1, source_target_pairs={{0,1},{1,0},{2,3},{3,2},{4,5},{5,4},{6,7},{7,6},{8,9},{9,8},{10,11... | collective-permute-start | bytes 1572872 | tf_op jit(solution)/shard_map/ppermute | solution.py:396
  151.6 22.0 %copy-start.32 = (bf16[256,2048]{1,0:T(8,128)(2,1)}, bf16[256,2048]{1,0:T(8,128)(2,1)S(1)}, u32[]{:S(2)}) copy-start(bf16[256,2048]{1,0:T(8,128)(2,1)S(1)} %fusion.6) | copy-start | bytes 3145732
  153.0 23.7 %collective-permute-start.15 = (bf16[1024,1024]{1,0:T(8,128)(2,1)S(1)}, bf16[1024,1024]{1,0:T(8,128)(2,1)S(1)}, u32[]{:S(2)}, u32[]{:S(2)}) collective-permute-start(bf16[1024,1024]{1,0:T(8,128)(2,1)S(1)} %convolution_convert_fusion.2), channel_id=1, source_target_pairs={{0,4},{4,0},{8,12},{12,8},{16,20},{20,16},{24,28},{28,24},{1,5},{5... | collective-permute-start | bytes 6291464 | tf_op jit(solution)/shard_map/ppermute | solution.py:396
  154.4 19.2 %collective-permute-start.14 = (bf16[512,2048]{1,0:T(8,128)(2,1)S(1)}, bf16[512,2048]{1,0:T(8,128)(2,1)S(1)}, u32[]{:S(2)}, u32[]{:S(2)}) collective-permute-start(bf16[512,2048]{1,0:T(8,128)(2,1)S(1)} %convolution_convert_fusion), channel_id=1, source_target_pairs={{0,4},{4,0},{8,12},{12,8},{16,20},{20,16},{24,28},{28,24},{1,5},{5... | collective-permute-start | bytes 6291464 | tf_op jit(solution)/shard_map/ppermute | solution.py:396
  160.3 6.3 %collective-permute-start.11 = (bf16[256,256]{1,0:T(8,128)(2,1)S(1)}, bf16[256,256]{1,0:T(8,128)(2,1)S(1)}, u32[]{:S(2)}, u32[]{:S(2)}) collective-permute-start(bf16[256,256]{1,0:T(8,128)(2,1)S(1)} %get-tuple-element.150), channel_id=1, source_target_pairs={{0,1},{1,0},{2,3},{3,2},{4,5},{5,4},{6,7},{7,6},{8,9},{9,8},{10,11... | collective-permute-start | bytes 393224 | tf_op jit(solution)/shard_map/ppermute | solution.py:396
  161.5 11.9 %collective-permute-start.12 = (bf16[256,256]{1,0:T(8,128)(2,1)S(1)}, bf16[256,256]{1,0:T(8,128)(2,1)S(1)}, u32[]{:S(2)}, u32[]{:S(2)}) collective-permute-start(bf16[256,256]{1,0:T(8,128)(2,1)S(1)} %get-tuple-element.149), channel_id=1, source_target_pairs={{0,2},{1,3},{2,0},{3,1},{4,6},{5,7},{6,4},{7,5},{8,10},{9,11},{10,... | collective-permute-start | bytes 393224 | tf_op jit(solution)/shard_map/ppermute | solution.py:396
  163.3 10.1 %collective-permute-start.13 = (bf16[256,256]{1,0:T(8,128)(2,1)S(1)}, bf16[256,256]{1,0:T(8,128)(2,1)S(1)}, u32[]{:S(2)}, u32[]{:S(2)}) collective-permute-start(bf16[256,256]{1,0:T(8,128)(2,1)S(1)} %get-tuple-element.148), channel_id=1, source_target_pairs={{0,3},{1,2},{2,1},{3,0},{4,7},{5,6},{6,5},{7,4},{8,11},{9,10},{10,... | collective-permute-start | bytes 393224 | tf_op jit(solution)/shard_map/ppermute | solution.py:396
  166.7 29.5 %collective-permute-start.18 = (bf16[512,1024]{1,0:T(8,128)(2,1)S(1)}, bf16[512,1024]{1,0:T(8,128)(2,1)S(1)}, u32[]{:S(2)}, u32[]{:S(2)}) collective-permute-start(bf16[512,1024]{1,0:T(8,128)(2,1)S(1)} %bitcast.207), channel_id=1, source_target_pairs={{0,4},{4,0},{8,12},{12,8},{16,20},{20,16},{24,28},{28,24},{1,5},{5... | collective-permute-start | bytes 3145736 | tf_op jit(solution)/shard_map/ppermute | solution.py:396
  175.1 23.4 %collective-permute-start.17 = (bf16[256,2048]{1,0:T(8,128)(2,1)S(1)}, bf16[256,2048]{1,0:T(8,128)(2,1)S(1)}, u32[]{:S(2)}, u32[]{:S(2)}) collective-permute-start(bf16[256,2048]{1,0:T(8,128)(2,1)S(1)} %bitcast.209), channel_id=1, source_target_pairs={{0,16},{4,20},{8,24},{12,28},{16,0},{20,4},{24,8},{28,12},{1,17},{... | collective-permute-start | bytes 3145736 | tf_op jit(solution)/shard_map/ppermute | solution.py:396
  178.1 24.8 %collective-permute-start.16 = (bf16[512,1024]{1,0:T(8,128)(2,1)S(1)}, bf16[512,1024]{1,0:T(8,128)(2,1)S(1)}, u32[]{:S(2)}, u32[]{:S(2)}) collective-permute-start(bf16[512,1024]{1,0:T(8,128)(2,1)S(1)} %bitcast.210), channel_id=1, source_target_pairs={{0,8},{4,12},{8,0},{12,4},{16,24},{20,28},{24,16},{28,20},{1,9},{5... | collective-permute-start | bytes 3145736 | tf_op jit(solution)/shard_map/ppermute | solution.py:396
  196.7 25.5 %collective-permute-start.21 = (bf16[256,1024]{1,0:T(8,128)(2,1)S(1)}, bf16[256,1024]{1,0:T(8,128)(2,1)S(1)}, u32[]{:S(2)}, u32[]{:S(2)}) collective-permute-start(bf16[256,1024]{1,0:T(8,128)(2,1)S(1)} %bitcast.217), channel_id=1, source_target_pairs={{0,8},{4,12},{8,0},{12,4},{16,24},{20,28},{24,16},{28,20},{1,9},{5... | collective-permute-start | bytes 1572872 | tf_op jit(solution)/shard_map/ppermute | solution.py:396
  203.9 20.4 %collective-permute-start.20 = (bf16[128,2048]{1,0:T(8,128)(2,1)S(1)}, bf16[128,2048]{1,0:T(8,128)(2,1)S(1)}, u32[]{:S(2)}, u32[]{:S(2)}) collective-permute-start(bf16[128,2048]{1,0:T(8,128)(2,1)S(1)} %dynamic-slice_bitcast_fusion.1), channel_id=1, source_target_pairs={{0,8},{4,12},{8,0},{12,4},{16,24},{20,28},{24,16},{28,20},{1,9},{5... | collective-permute-start | bytes 1572872 | tf_op jit(solution)/shard_map/ppermute | solution.py:396
  221.1 9.2 %collective-permute-start.19 = (bf16[256,1024]{1,0:T(8,128)(2,1)S(1)}, bf16[256,1024]{1,0:T(8,128)(2,1)S(1)}, u32[]{:S(2)}, u32[]{:S(2)}) collective-permute-start(bf16[256,1024]{1,0:T(8,128)(2,1)S(1)} %bitcast.216), channel_id=1, source_target_pairs={{0,16},{4,20},{8,24},{12,28},{16,0},{20,4},{24,8},{28,12},{1,17},{... | collective-permute-start | bytes 1572872 | tf_op jit(solution)/shard_map/ppermute | solution.py:396
  222.5 23.8 %collective-permute-start.22 = (bf16[128,1024]{1,0:T(8,128)(2,1)S(1)}, bf16[128,1024]{1,0:T(8,128)(2,1)S(1)}, u32[]{:S(2)}, u32[]{:S(2)}) collective-permute-start(bf16[128,1024]{1,0:T(8,128)(2,1)S(1)} %bitcast.221), channel_id=1, source_target_pairs={{0,16},{4,20},{8,24},{12,28},{16,0},{20,4},{24,8},{28,12},{1,17},{... | collective-permute-start | bytes 786440 | tf_op jit(solution)/shard_map/ppermute | solution.py:396
  224.2 12.0 %copy-start.14 = (bf16[2,1024,1024]{2,1,0:T(8,128)(2,1)S(1)}, bf16[2,1024,1024]{2,1,0:T(8,128)(2,1)}, u32[]{:S(2)}) copy-start(bf16[2,1024,1024]{2,1,0:T(8,128)(2,1)} %get-tuple-element.72.refs_2_) | copy-start | bytes 12582916
  224.4 11.8 %copy-start.11 = (bf16[2048,256]{1,0:T(8,128)(2,1)S(1)}, bf16[2048,256]{1,0:T(8,128)(2,1)}, u32[]{:S(2)}) copy-start(bf16[2048,256]{1,0:T(8,128)(2,1)} %fusion.3.refs_1_) | copy-start | bytes 3145732
  230.6 32.1 %collective-permute-start.23 = (bf16[256,1024]{1,0:T(8,128)(2,1)S(1)}, bf16[256,1024]{1,0:T(8,128)(2,1)S(1)}, u32[]{:S(2)}, u32[]{:S(2)}) collective-permute-start(bf16[256,1024]{1,0:T(8,128)(2,1)S(1)} %pad_maximum_fusion.18), channel_id=1, source_target_pairs={{0,2},{1,3},{2,0},{3,1},{4,6},{5,7},{6,4},{7,5},{8,10},{9,11},{10,... | collective-permute-start | bytes 1572872 | tf_op jit(solution)/shard_map/ppermute | solution.py:396
  236.2 14.6 %copy-start.15 = (bf16[2,1024,1024]{2,1,0:T(8,128)(2,1)S(1)}, bf16[2,1024,1024]{2,1,0:T(8,128)(2,1)}, u32[]{:S(2)}) copy-start(bf16[2,1024,1024]{2,1,0:T(8,128)(2,1)} %get-tuple-element.79.refs_2_) | copy-start | bytes 12582916
  246.3 14.6 %copy-start.22 = (bf16[128,2048]{1,0:T(8,128)(2,1)}, bf16[128,2048]{1,0:T(8,128)(2,1)S(1)}, u32[]{:S(2)}) copy-start(bf16[128,2048]{1,0:T(8,128)(2,1)S(1)} %get-tuple-element.89.refs_7_) | copy-start | bytes 1572868
  246.4 16.2 %collective-permute-start.24 = (bf16[32,1024]{1,0:T(8,128)(2,1)S(1)}, bf16[32,1024]{1,0:T(8,128)(2,1)S(1)}, u32[]{:S(2)}, u32[]{:S(2)}) collective-permute-start(bf16[32,1024]{1,0:T(8,128)(2,1)S(1)} %get-tuple-element.159), channel_id=1, source_target_pairs={{0,1},{1,0},{2,3},{3,2},{4,5},{5,4},{6,7},{7,6},{8,9},{9,8},{10,11... | collective-permute-start | bytes 196616 | tf_op jit(solution)/shard_map/ppermute | solution.py:396
  246.8 15.8 %collective-permute-start.25 = (bf16[32,1024]{1,0:T(8,128)(2,1)S(1)}, bf16[32,1024]{1,0:T(8,128)(2,1)S(1)}, u32[]{:S(2)}, u32[]{:S(2)}) collective-permute-start(bf16[32,1024]{1,0:T(8,128)(2,1)S(1)} %get-tuple-element.160), channel_id=1, source_target_pairs={{0,2},{1,3},{2,0},{3,1},{4,6},{5,7},{6,4},{7,5},{8,10},{9,11},{10,... | collective-permute-start | bytes 196616 | tf_op jit(solution)/shard_map/ppermute | solution.py:396
  249.7 13.0 %collective-permute-start.26 = (bf16[32,1024]{1,0:T(8,128)(2,1)S(1)}, bf16[32,1024]{1,0:T(8,128)(2,1)S(1)}, u32[]{:S(2)}, u32[]{:S(2)}) collective-permute-start(bf16[32,1024]{1,0:T(8,128)(2,1)S(1)} %slice_bitcast_fusion.3), channel_id=1, source_target_pairs={{0,3},{1,2},{2,1},{3,0},{4,7},{5,6},{6,5},{7,4},{8,11},{9,10},{10,... | collective-permute-start | bytes 196616 | tf_op jit(solution)/shard_map/ppermute | solution.py:396
  263.9 110.5 %reduce-scatter.2.cloned.1.call-start = ((), (), s32[]{:S(2)}) async-start(), calls=%async_computation.1 | async-start | bytes 2621440 | tf_op jit(solution)/shard_map/reduce_scatter | solution.py:751
  278.5 2.9 collective-permute-start.27
  283.3 14.4 %collective-permute-start.28 = (bf16[144,1024]{1,0:T(8,128)(2,1)S(1)}, bf16[144,1024]{1,0:T(8,128)(2,1)S(1)}, u32[]{:S(2)}, u32[]{:S(2)}) collective-permute-start(bf16[144,1024]{1,0:T(8,128)(2,1)S(1)} %get-tuple-element.127), channel_id=1, source_target_pairs={{0,8},{4,12},{8,0},{12,4},{16,24},{20,28},{24,16},{28,20},{1,9},{5... | collective-permute-start | bytes 884744 | tf_op jit(solution)/shard_map/ppermute | solution.py:396
  284.7 17.6 %collective-permute-start.29 = (bf16[144,1024]{1,0:T(8,128)(2,1)S(1)}, bf16[144,1024]{1,0:T(8,128)(2,1)S(1)}, u32[]{:S(2)}, u32[]{:S(2)}) collective-permute-start(bf16[144,1024]{1,0:T(8,128)(2,1)S(1)} %get-tuple-element.129), channel_id=1, source_target_pairs={{0,16},{4,20},{8,24},{12,28},{16,0},{20,4},{24,8},{28,12},{1,17},{... | collective-permute-start | bytes 884744 | tf_op jit(solution)/shard_map/ppermute | solution.py:396
  286.1 23.9 %collective-permute-start.30 = (bf16[144,1024]{1,0:T(8,128)(2,1)S(1)}, bf16[144,1024]{1,0:T(8,128)(2,1)}, u32[]{:S(2)}, u32[]{:S(2)}) collective-permute-start(bf16[144,1024]{1,0:T(8,128)(2,1)S(1)} %get-tuple-element.128), channel_id=1, source_target_pairs={{0,24},{4,28},{8,16},{12,20},{16,8},{20,12},{24,0},{28,4},{1,25},{... | collective-permute-start | bytes 884744 | tf_op jit(solution)/shard_map/ppermute | solution.py:396
  311.2 14.8 %copy-start.68 = (bf16[1024,256]{1,0:T(8,128)(2,1)S(1)}, bf16[1024,256]{1,0:T(8,128)(2,1)}, u32[]{:S(2)}) copy-start(bf16[1024,256]{1,0:T(8,128)(2,1)} %param.25) | copy-start | bytes 1572868
  311.2 14.8 %copy-start.70 = (bf16[1024,256]{1,0:T(8,128)(2,1)S(1)}, bf16[1024,256]{1,0:T(8,128)(2,1)}, u32[]{:S(2)}) copy-start(bf16[1024,256]{1,0:T(8,128)(2,1)} %param.27) | copy-start | bytes 1572868
  311.2 14.8 %copy-start.72 = (bf16[1024,256]{1,0:T(8,128)(2,1)S(1)}, bf16[1024,256]{1,0:T(8,128)(2,1)}, u32[]{:S(2)}) copy-start(bf16[1024,256]{1,0:T(8,128)(2,1)} %param.29) | copy-start | bytes 1572868
  313.0 5.4 %collective-permute-start.31 = (bf16[80,1024]{1,0:T(8,128)(2,1)S(1)}, bf16[80,1024]{1,0:T(8,128)(2,1)S(1)}, u32[]{:S(2)}, u32[]{:S(2)}) collective-permute-start(bf16[80,1024]{1,0:T(8,128)(2,1)S(1)} %pad_maximum_fusion.21), channel_id=1, source_target_pairs={{0,1},{1,0},{2,3},{3,2},{4,5},{5,4},{6,7},{7,6},{8,9},{9,8},{10,11... | collective-permute-start | bytes 491528 | tf_op jit(solution)/shard_map/ppermute | solution.py:396
  318.4 7.5 %collective-permute-start.32 = (bf16[80,1024]{1,0:T(8,128)(2,1)S(1)}, bf16[80,1024]{1,0:T(8,128)(2,1)S(1)}, u32[]{:S(2)}, u32[]{:S(2)}) collective-permute-start(bf16[80,1024]{1,0:T(8,128)(2,1)S(1)} %add_convert_fusion.9), channel_id=1, source_target_pairs={{0,2},{1,3},{2,0},{3,1},{4,6},{5,7},{6,4},{7,5},{8,10},{9,11},{10,... | collective-permute-start | bytes 491528 | tf_op jit(solution)/shard_map/ppermute | solution.py:396
  330.7 10.8 %collective-permute-start.33 = (bf16[176,1024]{1,0:T(8,128)(2,1)S(1)}, bf16[176,1024]{1,0:T(8,128)(2,1)S(1)}, u32[]{:S(2)}, u32[]{:S(2)}) collective-permute-start(bf16[176,1024]{1,0:T(8,128)(2,1)S(1)} %get-tuple-element.156), channel_id=1, source_target_pairs={{0,8},{4,12},{8,0},{12,4},{16,24},{20,28},{24,16},{28,20},{1,9},{5... | collective-permute-start | bytes 1081352 | tf_op jit(solution)/shard_map/ppermute | solution.py:396
  333.3 13.4 %collective-permute-start.34 = (bf16[176,1024]{1,0:T(8,128)(2,1)S(1)}, bf16[176,1024]{1,0:T(8,128)(2,1)S(1)}, u32[]{:S(2)}, u32[]{:S(2)}) collective-permute-start(bf16[176,1024]{1,0:T(8,128)(2,1)S(1)} %get-tuple-element.156), channel_id=1, source_target_pairs={{0,16},{4,20},{8,24},{12,28},{16,0},{20,4},{24,8},{28,12},{1,17},{... | collective-permute-start | bytes 1081352 | tf_op jit(solution)/shard_map/ppermute | solution.py:396
  334.8 12.0 %collective-permute-start.35 = (bf16[176,1024]{1,0:T(8,128)(2,1)S(1)}, bf16[176,1024]{1,0:T(8,128)(2,1)S(1)}, u32[]{:S(2)}, u32[]{:S(2)}) collective-permute-start(bf16[176,1024]{1,0:T(8,128)(2,1)S(1)} %get-tuple-element.156), channel_id=1, source_target_pairs={{0,24},{4,28},{8,16},{12,20},{16,8},{20,12},{24,0},{28,4},{1,25},{... | collective-permute-start | bytes 1081352 | tf_op jit(solution)/shard_map/ppermute | solution.py:396
  354.8 3.2 collective-permute-start.36
  359.0 15.4 %copy-start.27 = (f32[256,1024]{1,0:T(8,128)S(1)}, f32[256,1024]{1,0:T(8,128)}, u32[]{:S(2)}) copy-start(f32[256,1024]{1,0:T(8,128)} %copy-done.26) | copy-start | bytes 3145732
  359.0 17.5 %copy-start.1 = (bf16[256,1024]{1,0:T(8,128)(2,1)S(1)}, bf16[256,1024]{1,0:T(8,128)(2,1)}, u32[]{:S(2)}) copy-start(bf16[256,1024]{1,0:T(8,128)(2,1)} %param.31) | copy-start | bytes 1572868
  (56 other events, 183.4 us)
Sparse Core Ops, SparseCore 0:
  20.8 27.3 all-gather.6
  51.9 36.8 all-gather.8
  264.0 50.2 all-gather.10
  330.8 43.5 reduce-scatter.1
